TPU v7x, 512 devices: a whole 4x8x8 slice. The times are simulated.
512 devices in a mesh: dp: 8 (over z_lo, x), space: 64 (over z_hi, y, core).
Axes of the slice: x: 4, y: 8, z: 8 (z_hi: 4, z_lo: 2; z = z_hi * 2 + z_lo), core: 2. Of those that a mesh axis runs over, the one named last changes fastest.
Arguments:
- volume_in: float32 [8, 64, 4, 64, 216], P('dp', 'space'), may hold values from -6 to 6
- filter_one: float32 [27, 16, 4], replicated, may hold values from -0.625 to 0.625
- filter_two: float32 [27, 32, 16], replicated, may hold values from -0.3125 to 0.3125
- out_grad: float32 [8, 64, 32, 216], P('dp', 'space'), may hold values from -6 to 6
Outputs:
- level_two: float32 [8, 64, 32, 216], P('dp', 'space')
- hidden_grad: float32 [8, 64, 16, 8, 216], P('dp', 'space')
- grad_one: float32 [27, 16, 4], replicated
- grad_two: float32 [27, 32, 16], replicated
All inputs are finite; a program needn't handle non-finite values.
Results may differ from a plain program's by a relative error of at most 0.0014.
Values sent between devices are 32-bit elements; how exact they have to be, the bound alone decides.
A program may use at most 64 MiB of HBM per device.

v0:
```python
import jax
import jax.numpy as jnp
from jax import lax
from jax.sharding import PartitionSpec as P

EDGE = 24


SLOPE = 0.3


def shifted(block, axis, distance):
    devices = range(lax.axis_size(axis))
    route = [(i - distance, i) for i in devices if i - distance in devices]
    return lax.ppermute(block, axis, route)


def lrelu(v):
    return jnp.where(v > 0, v, SLOPE * v)


def dslope(v):
    return jnp.where(v > 0, 1.0, SLOPE).astype(v.dtype)


def grid_place():
    grid_z = lax.axis_size("space") // 16
    where = lax.axis_index("space")
    coords = (where // (4 * grid_z), where // grid_z % 4, where % grid_z)
    return ((4 * grid_z, grid_z, 1), coords, (4, 4, grid_z))


def allowed(coord, limit, lower):
    flag = coord > 0 if lower else coord < limit - 1
    return flag.astype(jnp.float32)


def subset_list():
    return [(0,), (1,), (2,), (0, 1), (0, 2), (1, 2), (0, 1, 2)]


def cell_coords(side):
    index = jnp.arange(side**3)
    return (index // (side * side), index // side % side, index % side)


def pick_matrix(side, face_dims, lower):
    rest = [d for d in range(3) if d not in face_dims]
    count = side ** len(rest)
    cells = cell_coords(side)
    slots = jnp.arange(count)
    wanted = jnp.ones((side**3, count), bool)
    edge_value = side - 1 if lower else 0
    for d in face_dims:
        wanted = wanted & (cells[d] == edge_value)[:, None]
    for place, d in enumerate(rest):
        digit = slots // side ** (len(rest) - 1 - place) % side
        wanted = wanted & (cells[d][:, None] == digit[None, :])
    return wanted.astype(jnp.float32)


def place_matrix(side, face_dims, lower):
    rest = [d for d in range(3) if d not in face_dims]
    count = side ** len(rest)
    cells = cell_coords(side)
    slots = jnp.arange(count)
    wanted = jnp.ones((count, side**3), bool)
    edge_value = 0 if lower else side - 1
    for d in face_dims:
        wanted = wanted & (cells[d] == edge_value)[None, :]
    for place, d in enumerate(rest):
        digit = slots // side ** (len(rest) - 1 - place) % side
        wanted = wanted & (digit[:, None] == cells[d][None, :])
    return wanted.astype(jnp.float32)


def apply_matrix(field, matrix):
    return jnp.einsum("vcgq,qr->vcgr", field, matrix, precision=lax.Precision.HIGHEST)


def local_shift(field, side, shift_dims, lower):
    strides = (side * side, side, 1)
    amount = sum((strides[d] for d in shift_dims))
    cells = cell_coords(side)
    moved = jnp.roll(field, amount if lower else -amount, axis=3)
    inside = jnp.ones((side**3,), bool)
    for d in shift_dims:
        inside = inside & (cells[d] > 0 if lower else cells[d] < side - 1)
    return jnp.where(inside, moved, 0.0)


def neighbour_step(face_dims, lower):
    strides, coords, limits = grid_place()
    amount = sum((strides[d] for d in face_dims))
    valid = jnp.float32(1.0)
    for d in face_dims:
        valid = valid * allowed(coords[d], limits[d], lower)
    return (amount if lower else -amount, valid)


def take_groups(field, positions):
    if list(positions) == list(range(field.shape[2])):
        return field
    return jnp.concatenate([field[:, :, p : p + 1] for p in positions], axis=2)


def sets_sectioned(field, side, groups_for, lower):
    results = {(): field}
    members = {(): list(range(field.shape[2]))}
    for dims in subset_list():
        parent = dims[:-1]
        last = dims[-1]
        chosen = groups_for(dims)
        source = take_groups(results[parent], [members[parent].index(g) for g in chosen])
        face = apply_matrix(source, pick_matrix(side, (last,), lower))
        amount, valid = neighbour_step((last,), lower)
        moved = shifted(face, "space", amount) * valid
        filled = apply_matrix(moved, place_matrix(side, (last,), lower))
        results[dims] = local_shift(source, side, (last,), lower) + filled
        members[dims] = chosen
    return (results, members)


def shifted_sets(field, side, groups_for, lower):
    return sets_sectioned(field, side, groups_for, lower)


def groups_input(dims):
    return [
        g for g in range(64) if all((g >> 5 - d & 1 == 1 and g >> 2 - d & 1 == 1 for d in dims))
    ]


def groups_hidden(dims):
    return [g for g in range(8) if all((g >> 2 - d & 1 == 1 for d in dims))]


def groups_single(dims):
    return [0]


def offsets(k):
    return (k // 9, k // 3 % 3, k % 3)


def body(volume_in, filter_one, filter_two, out_grad):
    side = EDGE // 4
    field_in = volume_in[:, 0]
    grad_field = out_grad[:, 0]
    chans_in = field_in.shape[1]
    chans_one = filter_one.shape[1]
    chans_two = filter_two.shape[1]
    flat_one = jnp.transpose(filter_one, (1, 0, 2)).reshape(chans_one, 27 * chans_in)
    flat_two = jnp.transpose(filter_two, (1, 0, 2)).reshape(chans_two, 27 * chans_one)
    low_in, members_in = shifted_sets(field_in, side, groups_input, True)
    stacks_in = []
    pre_parts = []
    for parity in range(8):
        qbits = [parity >> 2 - d & 1 for d in range(3)]
        pieces = []
        for k in range(27):
            kd = offsets(k)
            pbits, sbits, dims = ([], [], [])
            for d in range(3):
                if kd[d] == 1:
                    pbits.append(0)
                    sbits.append(qbits[d])
                elif kd[d] == 2:
                    pbits.append(1)
                    sbits.append(qbits[d])
                else:
                    pbits.append(1)
                    sbits.append(1 - qbits[d])
                    if qbits[d] == 0:
                        dims.append(d)
            group = (
                (4 * pbits[0] + 2 * pbits[1] + pbits[2]) * 8
                + 4 * sbits[0]
                + 2 * sbits[1]
                + sbits[2]
            )
            dims = tuple(dims)
            pieces.append(low_in[dims][:, :, members_in[dims].index(group)])
        stacked = jnp.concatenate(pieces, axis=1)
        stacks_in.append(stacked)
        pre_parts.append(
            jnp.einsum("ok,vkq->voq", flat_one, stacked, precision=lax.Precision.HIGHEST)
        )
    pre_one = jnp.stack(pre_parts, axis=2)
    hidden = lrelu(pre_one)
    low_hidden, members_hidden = shifted_sets(hidden, side, groups_hidden, True)
    pieces = []
    for k in range(27):
        kd = offsets(k)
        sbits = [0 if kd[d] == 1 else 1 for d in range(3)]
        dims = tuple((d for d in range(3) if kd[d] == 0))
        group = 4 * sbits[0] + 2 * sbits[1] + sbits[2]
        pieces.append(low_hidden[dims][:, :, members_hidden[dims].index(group)])
    stack_hidden = jnp.concatenate(pieces, axis=1)
    pre_two = jnp.einsum("ok,vkq->voq", flat_two, stack_hidden, precision=lax.Precision.HIGHEST)
    act_two = lrelu(pre_two)
    delta_two = grad_field * dslope(pre_two)
    grad_two = jnp.einsum("voq,vkq->ok", delta_two, stack_hidden, precision=lax.Precision.HIGHEST)
    grad_two = jnp.transpose(grad_two.reshape(chans_two, 27, chans_one), (1, 0, 2))
    high_delta, members_delta = shifted_sets(delta_two[:, :, None], side, groups_single, False)
    back_parts = []
    for parity in range(8):
        qbits = [parity >> 2 - d & 1 for d in range(3)]
        total = None
        for k in range(27):
            kd = offsets(k)
            fits = all((kd[d] == 1 if qbits[d] == 0 else kd[d] != 1 for d in range(3)))
            if fits:
                dims = tuple((d for d in range(3) if kd[d] == 0))
                term = jnp.einsum(
                    "oc,voq->vcq",
                    filter_two[k],
                    high_delta[dims][:, :, 0],
                    precision=lax.Precision.HIGHEST,
                )
                total = term if total is None else total + term
        back_parts.append(total)
    back = jnp.stack(back_parts, axis=2)
    delta_one = back * dslope(pre_one)
    grad_one = None
    for parity in range(8):
        term = jnp.einsum(
            "voq,vkq->ok",
            delta_one[:, :, parity],
            stacks_in[parity],
            precision=lax.Precision.HIGHEST,
        )
        grad_one = term if grad_one is None else grad_one + term
    grad_one = jnp.transpose(grad_one.reshape(chans_one, 27, chans_in), (1, 0, 2))
    grad_one, grad_two = lax.psum((grad_one, grad_two), ("dp", "space"))
    return (act_two[:, None], back[:, None], grad_one, grad_two)


def solution(mesh):
    placed = (P("dp", "space", None, None, None), P(), P(), P("dp", "space", None, None))
    return jax.shard_map(
        body,
        mesh=mesh,
        in_specs=placed,
        out_specs=(P("dp", "space", None, None), P("dp", "space", None, None, None), P(), P()),
        check_vma=False,
    )
```

profile of v0, /device:TPU:1, one launch (start us, length us, event | category | flops | bytes accessed | tf_op | source)
XLA Modules:
  0.0 230.7 jit_solution(5670177494278646594)
XLA Ops:
  0.7 1.1 squeeze.661
  2.2 6.6 %collective-permute-start = (f32[1,4,16,36]{3,2,1,0:T(8,128)S(1)}, f32[1,4,16,36]{3,2,1,0:T(8,128)S(1)}, u32[]{:S(2)}, u32[]{:S(2)}) collective-permute-start(f32[1,4,16,36]{3,2,1,0:T(8,128)S(1)} %convolution_bitcast_fusion.7), channel_id=1, source_target_pairs={{0,16},{1,17},{2,18},{3,19},{4,20},{5,21},{6,22},{7,23},{8,24},{9,... | collective-permute-start | bytes 27656 | tf_op jit(solution)/shard_map/ppermute | solution.py:15
  8.8 1.0 fusion.295
  10.1 4.2 %collective-permute-start.4 = (f32[1,4,16,36]{3,2,1,0:T(8,128)S(1)}, f32[1,4,16,36]{3,2,1,0:T(8,128)S(1)}, u32[]{:S(2)}, u32[]{:S(2)}) collective-permute-start(f32[1,4,16,36]{3,2,1,0:T(8,128)S(1)} %convolution_bitcast_fusion.6), channel_id=1, source_target_pairs={{0,4},{1,5},{2,6},{3,7},{4,8},{5,9},{6,10},{7,11},{8,12},{9,13},{1... | collective-permute-start | bytes 27656 | tf_op jit(solution)/shard_map/ppermute | solution.py:15
  14.8 4.3 %collective-permute-start.6 = (f32[1,4,16,36]{3,2,1,0:T(8,128)S(1)}, f32[1,4,16,36]{3,2,1,0:T(8,128)S(1)}, u32[]{:S(2)}, u32[]{:S(2)}) collective-permute-start(f32[1,4,16,36]{3,2,1,0:T(8,128)S(1)} %convolution_bitcast_fusion.5), channel_id=1, source_target_pairs={{0,1},{1,2},{2,3},{3,4},{4,5},{5,6},{6,7},{7,8},{8,9},{9,10},{10,1... | collective-permute-start | bytes 27656 | tf_op jit(solution)/shard_map/ppermute | solution.py:15
  22.4 4.5 %collective-permute-start.1 = (f32[1,4,4,36]{3,2,1,0:T(4,128)S(1)}, f32[1,4,4,36]{3,2,1,0:T(4,128)S(1)}, u32[]{:S(2)}, u32[]{:S(2)}) collective-permute-start(f32[1,4,4,36]{3,2,1,0:T(4,128)S(1)} %convolution_bitcast_fusion.30), channel_id=1, source_target_pairs={{0,4},{1,5},{2,6},{3,7},{4,8},{5,9},{6,10},{7,11},{8,12},{9,13},{1... | collective-permute-start | bytes 6920 | tf_op jit(solution)/shard_map/ppermute | solution.py:15
  27.3 2.2 collective-permute-start.3
  29.6 2.4 %collective-permute-start.5 = (f32[1,4,4,36]{3,2,1,0:T(4,128)S(1)}, f32[1,4,4,36]{3,2,1,0:T(4,128)S(1)}, u32[]{:S(2)}, u32[]{:S(2)}) collective-permute-start(f32[1,4,4,36]{3,2,1,0:T(4,128)S(1)} %convolution_bitcast_fusion.28), channel_id=1, source_target_pairs={{0,1},{1,2},{2,3},{3,4},{4,5},{5,6},{6,7},{7,8},{8,9},{9,10},{10,1... | collective-permute-start | bytes 6920 | tf_op jit(solution)/shard_map/ppermute | solution.py:15
  32.4 2.6 %collective-permute-start.2 = (f32[1,4,1,36]{3,1,2,0:T(4,128)S(1)}, f32[1,4,1,36]{3,1,2,0:T(4,128)S(1)}, u32[]{:S(2)}, u32[]{:S(2)}) collective-permute-start(f32[1,4,1,36]{3,1,2,0:T(4,128)S(1)} %convolution_bitcast_fusion.31), channel_id=1, source_target_pairs={{0,1},{1,2},{2,3},{3,4},{4,5},{5,6},{6,7},{7,8},{8,9},{9,10},{10,1... | collective-permute-start | bytes 1736 | tf_op jit(solution)/shard_map/ppermute | solution.py:15
  42.0 7.2 %collective-permute-start.7 = (f32[1,16,4,36]{3,1,2,0:T(8,128)S(1)}, f32[1,16,4,36]{3,1,2,0:T(8,128)S(1)}, u32[]{:S(2)}, u32[]{:S(2)}) collective-permute-start(f32[1,16,4,36]{3,1,2,0:T(8,128)S(1)} %convolution_bitcast_fusion.4), channel_id=1, source_target_pairs={{0,16},{1,17},{2,18},{3,19},{4,20},{5,21},{6,22},{7,23},{8,24},{9,... | collective-permute-start | bytes 27656 | tf_op jit(solution)/shard_map/ppermute | solution.py:15
  49.3 2.8 %collective-permute-start.11 = (f32[1,16,4,36]{3,1,2,0:T(8,128)S(1)}, f32[1,16,4,36]{3,1,2,0:T(8,128)S(1)}, u32[]{:S(2)}, u32[]{:S(2)}) collective-permute-start(f32[1,16,4,36]{3,1,2,0:T(8,128)S(1)} %convolution_bitcast_fusion.3), channel_id=1, source_target_pairs={{0,4},{1,5},{2,6},{3,7},{4,8},{5,9},{6,10},{7,11},{8,12},{9,13},{1... | collective-permute-start | bytes 27656 | tf_op jit(solution)/shard_map/ppermute | solution.py:15
  52.1 4.6 %collective-permute-start.13 = (f32[1,16,4,36]{3,1,2,0:T(8,128)S(1)}, f32[1,16,4,36]{3,1,2,0:T(8,128)S(1)}, u32[]{:S(2)}, u32[]{:S(2)}) collective-permute-start(f32[1,16,4,36]{3,1,2,0:T(8,128)S(1)} %convolution_bitcast_fusion.2), channel_id=1, source_target_pairs={{0,1},{1,2},{2,3},{3,4},{4,5},{5,6},{6,7},{7,8},{8,9},{9,10},{10,1... | collective-permute-start | bytes 27656 | tf_op jit(solution)/shard_map/ppermute | solution.py:15
  58.2 6.4 %collective-permute-start.8 = (f32[1,16,2,36]{3,1,2,0:T(8,128)S(1)}, f32[1,16,2,36]{3,1,2,0:T(8,128)S(1)}, u32[]{:S(2)}, u32[]{:S(2)}) collective-permute-start(f32[1,16,2,36]{3,1,2,0:T(8,128)S(1)} %convolution_bitcast_fusion.18), channel_id=1, source_target_pairs={{0,4},{1,5},{2,6},{3,7},{4,8},{5,9},{6,10},{7,11},{8,12},{9,13},{1... | collective-permute-start | bytes 13832 | tf_op jit(solution)/shard_map/ppermute | solution.py:15
  64.6 2.2 collective-permute-start.10
  66.8 3.3 %collective-permute-start.12 = (f32[1,16,2,36]{3,1,2,0:T(8,128)S(1)}, f32[1,16,2,36]{3,1,2,0:T(8,128)S(1)}, u32[]{:S(2)}, u32[]{:S(2)}) collective-permute-start(f32[1,16,2,36]{3,1,2,0:T(8,128)S(1)} %convolution_bitcast_fusion.16), channel_id=1, source_target_pairs={{0,1},{1,2},{2,3},{3,4},{4,5},{5,6},{6,7},{7,8},{8,9},{9,10},{10,1... | collective-permute-start | bytes 13832 | tf_op jit(solution)/shard_map/ppermute | solution.py:15
  70.9 2.2 collective-permute-start.9
  74.6 0.8 copy-done
  75.3 1.1 fusion.81
  77.5 2.1 collective-permute-start.14
  79.6 1.3 collective-permute-start.15
  80.9 1.3 collective-permute-start.17
  82.2 1.4 convolution_bitcast_fusion
  83.7 5.8 %collective-permute-done.15 = f32[1,32,1,36]{3,1,2,0:T(8,128)S(1)} collective-permute-done((f32[1,32,1,36]{3,1,2,0:T(8,128)S(1)}, f32[1,32,1,36]{3,1,2,0:T(8,128)S(1)}, u32[]{:S(2)}, u32[]{:S(2)}) %collective-permute-start.15) | collective-permute-done | bytes 4640 | tf_op jit(solution)/shard_map/ppermute | solution.py:15
  90.1 8.4 %collective-permute-done.17 = f32[1,32,1,36]{3,1,2,0:T(8,128)S(1)} collective-permute-done((f32[1,32,1,36]{3,1,2,0:T(8,128)S(1)}, f32[1,32,1,36]{3,1,2,0:T(8,128)S(1)}, u32[]{:S(2)}, u32[]{:S(2)}) %collective-permute-start.17) | collective-permute-done | bytes 4640 | tf_op jit(solution)/shard_map/ppermute | solution.py:15
  99.8 2.8 %collective-permute-start.16 = (f32[1,32,1,36]{3,1,2,0:T(8,128)S(1)}, f32[1,32,1,36]{3,1,2,0:T(8,128)S(1)}, u32[]{:S(2)}, u32[]{:S(2)}) collective-permute-start(f32[1,32,1,36]{3,1,2,0:T(8,128)S(1)} %convolution_bitcast_fusion.12), channel_id=1, source_target_pairs={{1,0},{2,1},{3,2},{4,3},{5,4},{6,5},{7,6},{8,7},{9,8},{10,9},{11,1... | collective-permute-start | bytes 13832 | tf_op jit(solution)/shard_map/ppermute | solution.py:15
  102.6 1.9 collective-permute-start.18
  104.6 1.3 collective-permute-start.19
  106.8 3.4 %collective-permute-done.19 = f32[1,32,1,36]{3,1,2,0:T(8,128)S(1)} collective-permute-done((f32[1,32,1,36]{3,1,2,0:T(8,128)S(1)}, f32[1,32,1,36]{3,1,2,0:T(8,128)S(1)}, u32[]{:S(2)}, u32[]{:S(2)}) %collective-permute-start.19) | collective-permute-done | bytes 4640 | tf_op jit(solution)/shard_map/ppermute | solution.py:15
  111.8 3.0 %collective-permute-start.20 = (f32[1,32,1,36]{3,1,2,0:T(8,128)S(1)}, f32[1,32,1,36]{3,1,2,0:T(8,128)S(1)}, u32[]{:S(2)}, u32[]{:S(2)}) collective-permute-start(f32[1,32,1,36]{3,1,2,0:T(8,128)S(1)} %convolution_bitcast_fusion.8), channel_id=1, source_target_pairs={{1,0},{2,1},{3,2},{4,3},{5,4},{6,5},{7,6},{8,7},{9,8},{10,9},{11,1... | collective-permute-start | bytes 13832 | tf_op jit(solution)/shard_map/ppermute | solution.py:15
  115.4 2.3 %collective-permute-done.20 = f32[1,32,1,36]{3,1,2,0:T(8,128)S(1)} collective-permute-done((f32[1,32,1,36]{3,1,2,0:T(8,128)S(1)}, f32[1,32,1,36]{3,1,2,0:T(8,128)S(1)}, u32[]{:S(2)}, u32[]{:S(2)}) %collective-permute-start.20) | collective-permute-done | bytes 4640 | tf_op jit(solution)/shard_map/ppermute | solution.py:15
  121.7 107.4 %all-reduce = (f32[27,16,4]{1,2,0:T(4,128)S(1)}, f32[27,32,16]{0,1,2:T(8,128)S(1)}) all-reduce(f32[27,16,4]{1,2,0:T(4,128)S(1)} %bitcast.1460, f32[27,32,16]{0,1,2:T(8,128)S(1)} %convolution_bitcast_fusion), channel_id=1, replica_groups=mesh['dp'=8,'space'=64] {'dp','space'}, use_global_device_ids=true, to_apply=%region_0.1 | all-reduce | flops 15552 | bytes 124416 | tf_op jit(solution)/shard_map/psum | solution.py:235
  229.9 0.9 copy.135
  (370 shorter events, 25.0 us)
Async XLA Ops:
  2.2 18.7 %collective-permute-start = (f32[1,4,16,36]{3,2,1,0:T(8,128)S(1)}, f32[1,4,16,36]{3,2,1,0:T(8,128)S(1)}, u32[]{:S(2)}, u32[]{:S(2)}) collective-permute-start(f32[1,4,16,36]{3,2,1,0:T(8,128)S(1)} %convolution_bitcast_fusion.7), channel_id=1, source_target_pairs={{0,16},{1,17},{2,18},{3,19},{4,20},{5,21},{6,22},{7,23},{8,24},{9,... | collective-permute-start | bytes 27656 | tf_op jit(solution)/shard_map/ppermute | solution.py:15
  10.1 11.4 %collective-permute-start.4 = (f32[1,4,16,36]{3,2,1,0:T(8,128)S(1)}, f32[1,4,16,36]{3,2,1,0:T(8,128)S(1)}, u32[]{:S(2)}, u32[]{:S(2)}) collective-permute-start(f32[1,4,16,36]{3,2,1,0:T(8,128)S(1)} %convolution_bitcast_fusion.6), channel_id=1, source_target_pairs={{0,4},{1,5},{2,6},{3,7},{4,8},{5,9},{6,10},{7,11},{8,12},{9,13},{1... | collective-permute-start | bytes 27656 | tf_op jit(solution)/shard_map/ppermute | solution.py:15
  14.8 12.1 %collective-permute-start.6 = (f32[1,4,16,36]{3,2,1,0:T(8,128)S(1)}, f32[1,4,16,36]{3,2,1,0:T(8,128)S(1)}, u32[]{:S(2)}, u32[]{:S(2)}) collective-permute-start(f32[1,4,16,36]{3,2,1,0:T(8,128)S(1)} %convolution_bitcast_fusion.5), channel_id=1, source_target_pairs={{0,1},{1,2},{2,3},{3,4},{4,5},{5,6},{6,7},{7,8},{8,9},{9,10},{10,1... | collective-permute-start | bytes 27656 | tf_op jit(solution)/shard_map/ppermute | solution.py:15
  19.9 0.8 copy-start.2
  22.4 9.5 %collective-permute-start.1 = (f32[1,4,4,36]{3,2,1,0:T(4,128)S(1)}, f32[1,4,4,36]{3,2,1,0:T(4,128)S(1)}, u32[]{:S(2)}, u32[]{:S(2)}) collective-permute-start(f32[1,4,4,36]{3,2,1,0:T(4,128)S(1)} %convolution_bitcast_fusion.30), channel_id=1, source_target_pairs={{0,4},{1,5},{2,6},{3,7},{4,8},{5,9},{6,10},{7,11},{8,12},{9,13},{1... | collective-permute-start | bytes 6920 | tf_op jit(solution)/shard_map/ppermute | solution.py:15
  27.3 8.0 %collective-permute-start.3 = (f32[1,4,4,36]{3,2,1,0:T(4,128)S(1)}, f32[1,4,4,36]{3,2,1,0:T(4,128)S(1)}, u32[]{:S(2)}, u32[]{:S(2)}) collective-permute-start(f32[1,4,4,36]{3,2,1,0:T(4,128)S(1)} %convolution_bitcast_fusion.29), channel_id=1, source_target_pairs={{0,1},{1,2},{2,3},{3,4},{4,5},{5,6},{6,7},{7,8},{8,9},{9,10},{10,1... | collective-permute-start | bytes 6920 | tf_op jit(solution)/shard_map/ppermute | solution.py:15
  29.6 5.5 %collective-permute-start.5 = (f32[1,4,4,36]{3,2,1,0:T(4,128)S(1)}, f32[1,4,4,36]{3,2,1,0:T(4,128)S(1)}, u32[]{:S(2)}, u32[]{:S(2)}) collective-permute-start(f32[1,4,4,36]{3,2,1,0:T(4,128)S(1)} %convolution_bitcast_fusion.28), channel_id=1, source_target_pairs={{0,1},{1,2},{2,3},{3,4},{4,5},{5,6},{6,7},{7,8},{8,9},{9,10},{10,1... | collective-permute-start | bytes 6920 | tf_op jit(solution)/shard_map/ppermute | solution.py:15
  32.4 3.4 %collective-permute-start.2 = (f32[1,4,1,36]{3,1,2,0:T(4,128)S(1)}, f32[1,4,1,36]{3,1,2,0:T(4,128)S(1)}, u32[]{:S(2)}, u32[]{:S(2)}) collective-permute-start(f32[1,4,1,36]{3,1,2,0:T(4,128)S(1)} %convolution_bitcast_fusion.31), channel_id=1, source_target_pairs={{0,1},{1,2},{2,3},{3,4},{4,5},{5,6},{6,7},{7,8},{8,9},{9,10},{10,1... | collective-permute-start | bytes 1736 | tf_op jit(solution)/shard_map/ppermute | solution.py:15
  42.0 14.8 %collective-permute-start.7 = (f32[1,16,4,36]{3,1,2,0:T(8,128)S(1)}, f32[1,16,4,36]{3,1,2,0:T(8,128)S(1)}, u32[]{:S(2)}, u32[]{:S(2)}) collective-permute-start(f32[1,16,4,36]{3,1,2,0:T(8,128)S(1)} %convolution_bitcast_fusion.4), channel_id=1, source_target_pairs={{0,16},{1,17},{2,18},{3,19},{4,20},{5,21},{6,22},{7,23},{8,24},{9,... | collective-permute-start | bytes 27656 | tf_op jit(solution)/shard_map/ppermute | solution.py:15
  49.3 8.3 %collective-permute-start.11 = (f32[1,16,4,36]{3,1,2,0:T(8,128)S(1)}, f32[1,16,4,36]{3,1,2,0:T(8,128)S(1)}, u32[]{:S(2)}, u32[]{:S(2)}) collective-permute-start(f32[1,16,4,36]{3,1,2,0:T(8,128)S(1)} %convolution_bitcast_fusion.3), channel_id=1, source_target_pairs={{0,4},{1,5},{2,6},{3,7},{4,8},{5,9},{6,10},{7,11},{8,12},{9,13},{1... | collective-permute-start | bytes 27656 | tf_op jit(solution)/shard_map/ppermute | solution.py:15
  52.1 18.0 %collective-permute-start.13 = (f32[1,16,4,36]{3,1,2,0:T(8,128)S(1)}, f32[1,16,4,36]{3,1,2,0:T(8,128)S(1)}, u32[]{:S(2)}, u32[]{:S(2)}) collective-permute-start(f32[1,16,4,36]{3,1,2,0:T(8,128)S(1)} %convolution_bitcast_fusion.2), channel_id=1, source_target_pairs={{0,1},{1,2},{2,3},{3,4},{4,5},{5,6},{6,7},{7,8},{8,9},{9,10},{10,1... | collective-permute-start | bytes 27656 | tf_op jit(solution)/shard_map/ppermute | solution.py:15
  58.2 12.3 %collective-permute-start.8 = (f32[1,16,2,36]{3,1,2,0:T(8,128)S(1)}, f32[1,16,2,36]{3,1,2,0:T(8,128)S(1)}, u32[]{:S(2)}, u32[]{:S(2)}) collective-permute-start(f32[1,16,2,36]{3,1,2,0:T(8,128)S(1)} %convolution_bitcast_fusion.18), channel_id=1, source_target_pairs={{0,4},{1,5},{2,6},{3,7},{4,8},{5,9},{6,10},{7,11},{8,12},{9,13},{1... | collective-permute-start | bytes 13832 | tf_op jit(solution)/shard_map/ppermute | solution.py:15
  64.6 8.6 %collective-permute-start.10 = (f32[1,16,2,36]{3,1,2,0:T(8,128)S(1)}, f32[1,16,2,36]{3,1,2,0:T(8,128)S(1)}, u32[]{:S(2)}, u32[]{:S(2)}) collective-permute-start(f32[1,16,2,36]{3,1,2,0:T(8,128)S(1)} %convolution_bitcast_fusion.17), channel_id=1, source_target_pairs={{0,1},{1,2},{2,3},{3,4},{4,5},{5,6},{6,7},{7,8},{8,9},{9,10},{10,1... | collective-permute-start | bytes 13832 | tf_op jit(solution)/shard_map/ppermute | solution.py:15
  66.8 6.6 %collective-permute-start.12 = (f32[1,16,2,36]{3,1,2,0:T(8,128)S(1)}, f32[1,16,2,36]{3,1,2,0:T(8,128)S(1)}, u32[]{:S(2)}, u32[]{:S(2)}) collective-permute-start(f32[1,16,2,36]{3,1,2,0:T(8,128)S(1)} %convolution_bitcast_fusion.16), channel_id=1, source_target_pairs={{0,1},{1,2},{2,3},{3,4},{4,5},{5,6},{6,7},{7,8},{8,9},{9,10},{10,1... | collective-permute-start | bytes 13832 | tf_op jit(solution)/shard_map/ppermute | solution.py:15
  70.9 3.1 %collective-permute-start.9 = (f32[1,16,1,36]{3,1,2,0:T(8,128)S(1)}, f32[1,16,1,36]{3,1,2,0:T(8,128)S(1)}, u32[]{:S(2)}, u32[]{:S(2)}) collective-permute-start(f32[1,16,1,36]{3,1,2,0:T(8,128)S(1)} %convolution_bitcast_fusion.27), channel_id=1, source_target_pairs={{0,1},{1,2},{2,3},{3,4},{4,5},{5,6},{6,7},{7,8},{8,9},{9,10},{10,1... | collective-permute-start | bytes 6920 | tf_op jit(solution)/shard_map/ppermute | solution.py:15
  74.4 0.9 copy-start
  74.5 0.8 copy-start.1
  77.5 21.9 %collective-permute-start.14 = (f32[1,32,1,36]{3,1,2,0:T(8,128)S(1)}, f32[1,32,1,36]{3,1,2,0:T(8,128)S(1)}, u32[]{:S(2)}, u32[]{:S(2)}) collective-permute-start(f32[1,32,1,36]{3,1,2,0:T(8,128)S(1)} %convolution_bitcast_fusion.14), channel_id=1, source_target_pairs={{1,0},{2,1},{3,2},{4,3},{5,4},{6,5},{7,6},{8,7},{9,8},{10,9},{11,1... | collective-permute-start | bytes 13832 | tf_op jit(solution)/shard_map/ppermute | solution.py:15
  79.6 9.8 %collective-permute-start.15 = (f32[1,32,1,36]{3,1,2,0:T(8,128)S(1)}, f32[1,32,1,36]{3,1,2,0:T(8,128)S(1)}, u32[]{:S(2)}, u32[]{:S(2)}) collective-permute-start(f32[1,32,1,36]{3,1,2,0:T(8,128)S(1)} %convolution_bitcast_fusion.13), channel_id=1, source_target_pairs={{4,0},{5,1},{6,2},{7,3},{8,4},{9,5},{10,6},{11,7},{12,8},{13,9},{1... | collective-permute-start | bytes 13832 | tf_op jit(solution)/shard_map/ppermute | solution.py:15
  80.9 17.6 %collective-permute-start.17 = (f32[1,32,1,36]{3,1,2,0:T(8,128)S(1)}, f32[1,32,1,36]{3,1,2,0:T(8,128)S(1)}, u32[]{:S(2)}, u32[]{:S(2)}) collective-permute-start(f32[1,32,1,36]{3,1,2,0:T(8,128)S(1)} %convolution_bitcast_fusion.11), channel_id=1, source_target_pairs={{16,0},{17,1},{18,2},{19,3},{20,4},{21,5},{22,6},{23,7},{24,8},{25... | collective-permute-start | bytes 13832 | tf_op jit(solution)/shard_map/ppermute | solution.py:15
  99.8 6.3 %collective-permute-start.16 = (f32[1,32,1,36]{3,1,2,0:T(8,128)S(1)}, f32[1,32,1,36]{3,1,2,0:T(8,128)S(1)}, u32[]{:S(2)}, u32[]{:S(2)}) collective-permute-start(f32[1,32,1,36]{3,1,2,0:T(8,128)S(1)} %convolution_bitcast_fusion.12), channel_id=1, source_target_pairs={{1,0},{2,1},{3,2},{4,3},{5,4},{6,5},{7,6},{8,7},{9,8},{10,9},{11,1... | collective-permute-start | bytes 13832 | tf_op jit(solution)/shard_map/ppermute | solution.py:15
  102.6 8.2 %collective-permute-start.18 = (f32[1,32,1,36]{3,1,2,0:T(8,128)S(1)}, f32[1,32,1,36]{3,1,2,0:T(8,128)S(1)}, u32[]{:S(2)}, u32[]{:S(2)}) collective-permute-start(f32[1,32,1,36]{3,1,2,0:T(8,128)S(1)} %convolution_bitcast_fusion.10), channel_id=1, source_target_pairs={{1,0},{2,1},{3,2},{4,3},{5,4},{6,5},{7,6},{8,7},{9,8},{10,9},{11,1... | collective-permute-start | bytes 13832 | tf_op jit(solution)/shard_map/ppermute | solution.py:15
  104.6 5.7 %collective-permute-start.19 = (f32[1,32,1,36]{3,1,2,0:T(8,128)S(1)}, f32[1,32,1,36]{3,1,2,0:T(8,128)S(1)}, u32[]{:S(2)}, u32[]{:S(2)}) collective-permute-start(f32[1,32,1,36]{3,1,2,0:T(8,128)S(1)} %convolution_bitcast_fusion.9), channel_id=1, source_target_pairs={{4,0},{5,1},{6,2},{7,3},{8,4},{9,5},{10,6},{11,7},{12,8},{13,9},{1... | collective-permute-start | bytes 13832 | tf_op jit(solution)/shard_map/ppermute | solution.py:15
  111.8 5.9 %collective-permute-start.20 = (f32[1,32,1,36]{3,1,2,0:T(8,128)S(1)}, f32[1,32,1,36]{3,1,2,0:T(8,128)S(1)}, u32[]{:S(2)}, u32[]{:S(2)}) collective-permute-start(f32[1,32,1,36]{3,1,2,0:T(8,128)S(1)} %convolution_bitcast_fusion.8), channel_id=1, source_target_pairs={{1,0},{2,1},{3,2},{4,3},{5,4},{6,5},{7,6},{8,7},{9,8},{10,9},{11,1... | collective-permute-start | bytes 13832 | tf_op jit(solution)/shard_map/ppermute | solution.py:15
where the time goes:
time: 232 us; the launch traced here: 231 us
  blocking collectives  107 us (46%)
  starting transfers between devices  69.4 us (30%)
  waiting for transfers between devices  20.4 us (9%)
  matrix products  19.5 us (8%)
  local copies, waits for them, and re-layouts  10.5 us (5%)
  between operations  2.8 us (1%)
    psum x1, blocking collectives, body(): grad_one, grad_two = lax.psum((grad_one, grad_two), ('dp', 'space'))  107 us
    ppermute x21, starting transfers between devices, shifted(): return lax.ppermute(block, axis, route)  69.4 us
    ppermute x21, waiting for transfers between devices, shifted(): return lax.ppermute(block, axis, route)  20.4 us
    dot_general x42, matrix products, apply_matrix(): jnp.einsum('vcgq,qr->vcgr', field, matrix, precision=lax.Precision.HIGHEST)  9.22 us
    unnamed x176, local copies, waits for them, and re-layouts  5.59 us
  transfers between devices with their start and end apart: 21, of which 6 were waited for; matrix products, arithmetic and copies ran while one was open for 6% of the time, Pallas kernels for 0%

commit v1 on v0

v1 whole, which is shorter than its diff:
```python
import itertools

import jax
import jax.numpy as jnp
import numpy as np
from jax import lax
from jax.experimental import pallas as pl
from jax.experimental.pallas import tpu as pltpu
from jax.sharding import PartitionSpec as P

SLOPE = 0.3
SIDE = 6
CELLS = SIDE**3
BF16 = jnp.bfloat16
F32 = jnp.float32
MESH = pl.DeviceIdType.MESH
HIGHEST = lax.Precision.HIGHEST

SUBSETS = [(0,), (1,), (2,), (0, 1), (0, 2), (1, 2), (0, 1, 2)]
SIZES = [SIDE ** (3 - len(s)) for s in SUBSETS]
STARTS = [sum(SIZES[:i]) for i in range(7)]


def rows_for(tiles):
    rows = [8 * -(-tiles // (128 // size)) for size in SIZES]
    return rows, [sum(rows[:i]) for i in range(7)]


IN_ROWS, IN_AT = rows_for(32)
D_ROWS, D_AT = rows_for(4)


def lane_of(coords, outside):
    dims = tuple(d for d in range(3) if coords[d] == outside)
    rest = [coords[d] for d in range(3) if d not in dims]
    place = 0
    for c in rest:
        place = place * SIDE + c
    return place if not dims else 256 + STARTS[SUBSETS.index(dims)] + place


def shift_matrices(step):
    outside = -1 if step < 0 else SIDE
    span = range(-1, SIDE) if step < 0 else range(SIDE + 1)
    m = np.zeros((3, 384, 384), np.float32)
    for coords in itertools.product(span, repeat=3):
        for d in range(3):
            source = list(coords)
            source[d] += step
            if coords[d] != outside:
                m[d, lane_of(source, outside), lane_of(coords, outside)] = 1
    return m


def pick_matrix(edge):
    m = np.zeros((256, 128), np.float32)
    for dims, start in zip(SUBSETS, STARTS):
        rest = [d for d in range(3) if d not in dims]
        for place, digits in enumerate(itertools.product(range(SIDE), repeat=len(rest))):
            coords = [edge] * 3
            for d, digit in zip(rest, digits):
                coords[d] = digit
            m[lane_of(coords, None), start + place] = 1
    return m


def spread_matrix():
    m = np.zeros((27, 432), np.float32)
    for k in range(27):
        m[k, 16 * k : 16 * k + 12] = 1
    return m


def iota(shape, dim):
    return lax.broadcasted_iota(jnp.int32, shape, dim)


def split(x, pieces):
    out = []
    for _ in range(pieces):
        piece = x.astype(BF16)
        out.append(piece)
        x = x - piece.astype(F32)
    return out


def dot(a, b, precision=None):
    return jnp.dot(a, b, preferred_element_type=F32, precision=precision)


def dot_t(a, b, precision=None):
    return lax.dot_general(a, b, (((1,), (1,)), ((), ())), preferred_element_type=F32, precision=precision)


def pack(tiles, buf, starts):
    lane = iota((8, 128), 1)
    for s in range(7):
        size = SIZES[s]
        per = 128 // size
        for block in range(-(-len(tiles) // per)):
            total = jnp.zeros((8, 128), F32)
            for i, tile in enumerate(tiles[block * per : (block + 1) * per]):
                moved = pltpu.roll(tile, (i * size - STARTS[s]) % 128, 1)
                total = jnp.where((lane >= i * size) & (lane < (i + 1) * size), moved, total)
            buf[starts[s] + 8 * block : starts[s] + 8 * block + 8, :] = total


def unpack(t, buf, starts, valid):
    lane = iota((8, 128), 1)
    total = jnp.zeros((8, 128), F32)
    for s in range(7):
        size = SIZES[s]
        per = 128 // size
        row = starts[s] + 8 * (t // per)
        moved = pltpu.roll(buf[row : row + 8, :], (STARTS[s] - (t % per) * size) % 128, 1)
        here = (lane >= STARTS[s]) & (lane < STARTS[s] + size) & (valid[s] > 0)
        total = jnp.where(here, moved, total)
    return total


def cell(i, j, l):
    return 16 * (25 * i + 5 * j + l)


def offsets(k):
    return (k // 9, k // 3 % 3, k % 3)


def bits(q):
    return (q >> 2 & 1, q >> 1 & 1, q & 1)


def level_kernel(
    x_ref, w1_ref, w2_ref, g_ref, low_ref, high_ref, pick_ref, pickl_ref, spread_ref,
    lev_ref, hid_ref, part_ref,
    xs, xc, hk, pre, back, send, recv, dsend, drecv, send_sem, recv_sem, dsend_sem, drecv_sem,
):
    where = lax.axis_index("space")
    coords = (where // 16, where // 4 % 4, where % 4)

    def neighbour(dims, step):
        moved = [(coords[d] + (step if d in dims else 0) + 4) % 4 for d in range(3)]
        return {"space": moved[0] * 16 + moved[1] * 4 + moved[2]}

    def flags(edge):
        inside = [jnp.where(coords[d] == edge, 0, 1) for d in range(3)]
        out = []
        for dims in SUBSETS:
            flag = 1
            for d in dims:
                flag = flag * inside[d]
            out.append(flag)
        return out

    barrier = pltpu.get_barrier_semaphore()
    for dims in SUBSETS:
        for step in (-1, 1):
            pl.semaphore_signal(barrier, inc=1, device_id=neighbour(dims, step), device_id_type=MESH)

    x = jnp.concatenate([x_ref[...], jnp.zeros((256, 40), F32)], axis=1)
    pieces = split(x, 3)
    picked = dot(pieces[0], pick_ref[...]) + dot(pieces[1], pick_ref[...])
    picked = picked + dot(pieces[2], pick_ref[...])
    pack([picked[8 * t : 8 * t + 8] for t in range(32)], send, IN_AT)
    pl.semaphore_wait(barrier, 14)
    copies = []
    for s, dims in enumerate(SUBSETS):
        rows = pl.ds(IN_AT[s], IN_ROWS[s])
        copies.append(
            pltpu.make_async_remote_copy(
                src_ref=send.at[rows],
                dst_ref=recv.at[rows],
                send_sem=send_sem.at[s],
                recv_sem=recv_sem.at[s],
                device_id=neighbour(dims, 1),
                device_id_type=MESH,
            )
        )
        copies[-1].start()

    w1 = dot(w1_ref[...], spread_ref[...], HIGHEST)
    w1 = jnp.where(iota((64, 432), 0) % 4 == iota((64, 432), 1) % 4, w1, 0.0)
    w1 = dot((iota((16, 64), 1) // 4 == iota((16, 64), 0)).astype(F32), w1, HIGHEST)
    slot = iota((16, 432), 1) // 4 % 4
    zero = jnp.zeros((16, 432), BF16)
    w1a, w1b, w1c = split(w1, 3)
    one_lhs = jnp.concatenate([w1a, jnp.where(slot < 2, w1b, zero), jnp.where(slot < 1, w1c, zero)], axis=0)
    eye = (iota((32, 32), 0) == iota((32, 32), 1)).astype(F32)
    two_lhs = jnp.concatenate(split(dot_t(eye, w2_ref[...], HIGHEST), 3), axis=0)
    back_rows = []
    for q in range(8):
        line = []
        for s in range(8):
            if s & ~q:
                line.append(jnp.zeros((16, 32), F32))
            else:
                k = 0
                for qb, sb in zip(bits(q), bits(s)):
                    k = 3 * k + (1 if qb == 0 else 0 if sb else 2)
                line.append(w2_ref[16 * k : 16 * k + 16, :])
        back_rows.append(jnp.concatenate(line, axis=1))
    back_lhs = jnp.concatenate(split(jnp.concatenate(back_rows, axis=0), 2), axis=0)

    for t in range(2):
        part = x[:, 128 * t : 128 * t + 128]
        xs[t, 0:256] = part
        xs[t, 256:512] = part
    upper = iota((8, 128), 0) < 4

    def gather(t):
        for g in range(64):
            index = [1 + 2 * (g >> (2 - d) & 1) + (g >> (5 - d) & 1) for d in range(3)]
            at = cell(*index)
            value = xs[t, pl.ds(g, 8, stride=64), :]
            hi, mid, lo = split(value, 3)
            first = jnp.where(upper, hi.astype(F32), mid.astype(F32))
            second = jnp.where(upper, lo.astype(F32), 0.0)
            xc[at : at + 16, 128 * t : 128 * t + 128] = jnp.concatenate([first, second], axis=0).astype(BF16)

    gather(0)
    gather(1)
    for copy in copies:
        copy.wait_recv()
    lower = flags(0)
    for t in range(32):
        tile = unpack(t, recv, IN_AT, lower)
        xs[2, 8 * t : 8 * t + 8] = tile
        xs[2, 256 + 8 * t : 264 + 8 * t] = tile
    gather(2)

    four, five = range(1, 5), range(5)
    for d, (ri, rj, rl) in enumerate([((4,), four, four), (five, (4,), four), (five, five, (4,))]):
        source = [cell(i, j, l) for i in ri for j in rj for l in rl]
        target = [at - cell(*[4 if e == d else 0 for e in range(3)]) for at in source]
        moved = dot(jnp.concatenate([xc[at : at + 16, :] for at in source], axis=0), low_ref[d]).astype(BF16)
        for n, at in enumerate(target):
            xc[at : at + 16, :] = moved[16 * n : 16 * n + 16]

    def stacked(q, lanes):
        b = bits(q)
        tiles = []
        for k in range(27):
            at = cell(*[2 * b[d] + offsets(k)[d] for d in range(3)])
            tiles.append(xc[at : at + 16, 0:lanes])
        return jnp.concatenate(tiles, axis=0)

    def three(k):
        return 16 * (9 * k[0] + 3 * k[1] + k[2])

    for q in range(8):
        r = dot(one_lhs, stacked(q, 384))
        value = (r[32:48] + r[16:32]) + r[0:16]
        pre[q] = value[:, 0:256]
        hidden = jnp.where(value > 0, value, SLOPE * value)
        at = three([1 + b for b in bits(q)])
        for n, piece in enumerate(split(hidden, 3)):
            hk[n, at : at + 16, :] = piece

    two = range(1, 3)
    for d, (ri, rj, rl) in enumerate([((2,), two, two), (range(3), (2,), two), (range(3), range(3), (2,))]):
        source = [three((i, j, l)) for i in ri for j in rj for l in rl]
        rows = jnp.concatenate([hk[n, at : at + 16, :] for n in range(3) for at in source], axis=0)
        lanes = 384 if d < 2 else 256
        moved = dot(rows, low_ref[d, :, 0:lanes]).astype(BF16)
        step = three([2 if e == d else 0 for e in range(3)])
        for n in range(3):
            for m, at in enumerate(source):
                row = 16 * (n * len(source) + m)
                hk[n, at - step : at - step + 16, 0:lanes] = moved[row : row + 16]

    r = dot(two_lhs, hk[0, :, 0:256])
    r2 = dot(two_lhs[0:64], hk[1, :, 0:256])
    r3 = dot(two_lhs[0:32], hk[2, :, 0:256])
    pre_two = ((r[64:96] + r2[32:64]) + r3 + (r[32:64] + r2[0:32])) + r[0:32]
    lev_ref[...] = jnp.where(pre_two > 0, pre_two, SLOPE * pre_two)[:, 0:CELLS]
    grad = jnp.concatenate([g_ref[...], jnp.zeros((32, 40), F32)], axis=1)
    delta = grad * jnp.where(pre_two > 0, 1.0, SLOPE)

    pieces = split(delta, 3)
    r = dot(jnp.concatenate(pieces, axis=0), pickl_ref[...])
    picked = (r[0:32] + r[32:64]) + r[64:96]
    pack([picked[8 * t : 8 * t + 8] for t in range(4)], dsend, D_AT)
    dcopies = []
    for s, dims in enumerate(SUBSETS):
        rows = pl.ds(D_AT[s], D_ROWS[s])
        dcopies.append(
            pltpu.make_async_remote_copy(
                src_ref=dsend.at[rows],
                dst_ref=drecv.at[rows],
                send_sem=dsend_sem.at[s],
                recv_sem=drecv_sem.at[s],
                device_id=neighbour(dims, -1),
                device_id_type=MESH,
            )
        )
        dcopies[-1].start()

    d1, d2 = pieces[0], pieces[1]
    r = dot_t(hk[0, :, 0:256], d1) + dot_t(hk[0, :, 0:256], d2) + dot_t(hk[1, :, 0:256], d1)
    r = jnp.concatenate([r, jnp.zeros((16, 32), F32)], axis=0)
    part_ref[0:112, :] = jnp.concatenate([r[112 * n : 112 * n + 112] for n in range(4)], axis=1)

    for copy in dcopies:
        copy.wait_recv()
    higher = flags(3)
    halo = jnp.concatenate([unpack(t, drecv, D_AT, higher) for t in range(4)], axis=0)
    both = jnp.concatenate(split(jnp.concatenate([delta, halo], axis=1), 2), axis=0)
    by_shift = {0: both}
    for d in range(3):
        bit = 4 >> d
        keys = sorted(by_shift)
        moved = dot(jnp.concatenate([by_shift[s] for s in keys], axis=0), high_ref[d]).astype(BF16)
        for n, s in enumerate(keys):
            by_shift[s | bit] = moved[64 * n : 64 * n + 64]
    da = jnp.concatenate([by_shift[s][0:32, 0:256] for s in range(8)], axis=0)
    db = jnp.concatenate([by_shift[s][32:64, 0:256] for s in range(8)], axis=0)
    r = dot(back_lhs, da)
    r = (r[128:256] + dot(back_lhs[0:128], db)) + r[0:128]
    total = None
    for q in range(8):
        value = r[16 * q : 16 * q + 16]
        for t in range(2):
            back[t, pl.ds(q, 16, stride=8), :] = value[:, 128 * t : 128 * t + 128]
        d_one = value * jnp.where(pre[q] > 0, 1.0, SLOPE)
        term = dot_t(stacked(q, 256), jnp.concatenate(split(d_one, 2), axis=0))
        total = term if total is None else total + term
    hid_ref[...] = jnp.concatenate([back[0], back[1]], axis=1)[:, 0:CELLS]

    lane, row = iota((8, 128), 1), iota((8, 128), 0)
    packed = [jnp.zeros((8, 128), F32), jnp.zeros((8, 128), F32)]
    for k in range(27):
        tile = jnp.concatenate([total[16 * k : 16 * k + 8], jnp.zeros((8, 96), F32)], axis=1)
        tile = tile + pltpu.roll(tile, 112, 1)
        tile = tile + pltpu.roll(tile, 4, 0)
        tile = pltpu.roll(tile, 16 * (k % 8), 1)
        here = (lane // 16 == k % 8) & (row // 4 == k // 8 % 2)
        packed[k // 16] = jnp.where(here, tile, packed[k // 16])
    part_ref[112:128, :] = jnp.concatenate(packed, axis=0)
    for copy in copies + dcopies:
        copy.wait_send()


def sum_kernel(part_ref, out_ref, ra, rb, mine, final, sem_a, sem_b, sem_c, out_a, out_b, out_c):
    dp, where = lax.axis_index("dp"), lax.axis_index("space")
    b, core = where // 2, where % 2
    a = dp * 2 + core

    def near(j):
        p = (a + j) % 16
        return p, {"dp": p // 2, "space": b * 2 + p % 2}

    def far(j):
        p = (b + j) % 32
        return p, {"space": p * 2 + core}

    barrier = pltpu.get_barrier_semaphore()
    for j in range(1, 16):
        pl.semaphore_signal(barrier, inc=1, device_id=near(j)[1], device_id_type=MESH)
    for j in range(1, 32):
        pl.semaphore_signal(barrier, inc=1, device_id=far(j)[1], device_id_type=MESH)
    pl.semaphore_wait(barrier, 46)

    def copy(src, dst, out_sem, in_sem, device):
        return pltpu.make_async_remote_copy(
            src_ref=src, dst_ref=dst, send_sem=out_sem, recv_sem=in_sem, device_id=device, device_id_type=MESH
        )

    first = []
    for j in range(1, 16):
        p, device = near(j)
        first.append(copy(part_ref.at[p], ra.at[a], out_a.at[j], sem_a.at[a], device))
        first[-1].start()
    ra[a] = part_ref[a]
    for j in range(1, 16):
        p, device = near(j)
        copy(part_ref.at[p], ra.at[p], out_a.at[j], sem_a.at[p], device).wait_recv()
    value = jnp.sum(ra[...], axis=0)
    mine[...] = value
    rb[b] = value
    second = []
    for j in range(1, 32):
        p, device = far(j)
        second.append(copy(mine, rb.at[b], out_b.at[j], sem_b.at[b], device))
        second[-1].start()
    for j in range(1, 32):
        p, device = far(j)
        copy(mine, rb.at[p], out_b.at[j], sem_b.at[p], device).wait_recv()
    value = jnp.sum(rb[...], axis=0)
    final[...] = value
    out_ref[a] = value
    third = []
    for j in range(1, 16):
        p, device = near(j)
        third.append(copy(final, out_ref.at[a], out_c.at[j], sem_c.at[a], device))
        third[-1].start()
    for j in range(1, 16):
        p, device = near(j)
        copy(final, out_ref.at[p], out_c.at[j], sem_c.at[p], device).wait_recv()
    for c in first + second + third:
        c.wait_send()


def body(volume_in, filter_one, filter_two, out_grad):
    vmem = pl.BlockSpec(memory_space=pltpu.VMEM)
    dma = pltpu.SemaphoreType.DMA
    constants = [
        jnp.asarray(shift_matrices(-1), BF16),
        jnp.asarray(shift_matrices(1), BF16),
        jnp.asarray(pick_matrix(SIDE - 1), BF16),
        jnp.asarray(pick_matrix(0), BF16),
        jnp.asarray(spread_matrix(), F32),
    ]
    level, hidden, part = pl.pallas_call(
        level_kernel,
        out_shape=[
            jax.ShapeDtypeStruct((32, CELLS), F32),
            jax.ShapeDtypeStruct((128, CELLS), F32),
            jax.ShapeDtypeStruct((128, 128), F32),
        ],
        in_specs=[vmem] * 9,
        out_specs=[vmem] * 3,
        scratch_shapes=[
            pltpu.VMEM((3, 512, 128), F32),
            pltpu.VMEM((2000, 384), BF16),
            pltpu.VMEM((3, 432, 384), BF16),
            pltpu.VMEM((8, 16, 256), F32),
            pltpu.VMEM((2, 128, 128), F32),
            pltpu.VMEM((sum(IN_ROWS), 128), F32),
            pltpu.VMEM((sum(IN_ROWS), 128), F32),
            pltpu.VMEM((sum(D_ROWS), 128), F32),
            pltpu.VMEM((sum(D_ROWS), 128), F32),
            dma((7,)),
            dma((7,)),
            dma((7,)),
            dma((7,)),
        ],
        compiler_params=pltpu.CompilerParams(
            collective_id=0, has_side_effects=True, vmem_limit_bytes=48 * 2**20
        ),
    )(
        volume_in.reshape(256, CELLS),
        jnp.transpose(filter_one, (1, 2, 0)).reshape(64, 27),
        jnp.transpose(filter_two, (0, 2, 1)).reshape(432, 32),
        out_grad.reshape(32, CELLS),
        *constants,
    )
    total = pl.pallas_call(
        sum_kernel,
        out_shape=jax.ShapeDtypeStruct((16, 8, 128), F32),
        in_specs=[vmem],
        out_specs=vmem,
        scratch_shapes=[
            pltpu.VMEM((16, 8, 128), F32),
            pltpu.VMEM((32, 8, 128), F32),
            pltpu.VMEM((8, 128), F32),
            pltpu.VMEM((8, 128), F32),
            dma((16,)),
            dma((32,)),
            dma((16,)),
            dma((16,)),
            dma((32,)),
            dma((16,)),
        ],
        compiler_params=pltpu.CompilerParams(
            collective_id=1, has_side_effects=True, vmem_limit_bytes=16 * 2**20
        ),
    )(part.reshape(16, 8, 128))
    total = total.reshape(128, 128)
    grad_two = total[0:112].reshape(7, 16, 4, 32)
    grad_two = jnp.transpose(grad_two, (2, 0, 1, 3)).reshape(28, 16, 32)[0:27]
    grad_one = total[112:128].reshape(4, 4, 8, 16)
    grad_one = jnp.transpose(grad_one, (0, 2, 1, 3)).reshape(32, 4, 16)[0:27]
    return (
        level.reshape(1, 1, 32, CELLS),
        hidden.reshape(1, 1, 16, 8, CELLS),
        jnp.transpose(grad_one, (0, 2, 1)),
        jnp.transpose(grad_two, (0, 2, 1)),
    )


def solution(mesh):
    placed = (P("dp", "space", None, None, None), P(), P(), P("dp", "space", None, None))
    return jax.shard_map(
        body,
        mesh=mesh,
        in_specs=placed,
        out_specs=(P("dp", "space", None, None), P("dp", "space", None, None, None), P(), P()),
        check_vma=False,
    )
```

time: 232 us -> 68.7 us (0.30)
  blocking collectives: 107 us -> 0 us
  starting transfers between devices: 69.4 us -> 0 us
  Pallas kernels: 0 us -> 55.5 us
  waiting for transfers between devices: 20.4 us -> 0 us
  matrix products: 19.5 us -> 0 us
    psum x1 -> x0, blocking collectives: 107 us -> none  [body(): grad_one, grad_two = lax.psum((grad_one, grad_two), ('dp', 'space'))]
    ppermute x21 -> x0, starting transfers between devices: 69.4 us -> none  [shifted(): return lax.ppermute(block, axis, route)]
    pallas_call x0 -> x2, Pallas kernels: none -> 55.5 us  [the longest x1 30.8 us: body(): pl.pallas_call(level_kernel, out_shape=[jax.ShapeDtypeStruct((32, CELLS),...]
    ppermute x21 -> x0, waiting for transfers between devices: 20.4 us -> none  [shifted(): return lax.ppermute(block, axis, route)]
    dot_general x87 -> x0, matrix products: 19.5 us -> none  [the longest x42 9.22 us: apply_matrix(): jnp.einsum('vcgq,qr->vcgr', field, matrix, precision=lax.Precision.HIGHEST)]
    unnamed x176 -> x23, local copies, waits for them, and re-layouts: 5.59 us -> 10.8 us
  transfers between devices with their start and end apart: 21 -> 0, of which waited for: 6 -> 0; matrix products, arithmetic and copies ran while one was open for 6% -> 0% of each run, Pallas kernels for 0% -> 0%
where the time goes in v1:
time: 68.7 us; the launch traced here: 68.1 us
  Pallas kernels  55.5 us (81%)
  local copies, waits for them, and re-layouts  11.9 us (17%)
  between operations  0.73 us (1%)
    pallas_call x1, Pallas kernels, body(): pl.pallas_call(level_kernel, out_shape=[jax.ShapeDtypeStruct((32, CELLS),...  30.8 us
    pallas_call x1, Pallas kernels, body(): pl.pallas_call(sum_kernel, out_shape=jax.ShapeDtypeStruct((16, 8, 128), F...  24.6 us
    unnamed x23, local copies, waits for them, and re-layouts  10.8 us

profile of v1, /device:TPU:1, one launch (start us, length us, event | category | flops | bytes accessed | tf_op | source)
XLA Modules:
  0.0 68.1 jit_solution(14154406296819593460)
XLA Ops:
  0.6 0.0 copy-start
  0.6 1.2 %copy-done = bf16[3,384,384]{2,1,0:T(8,128)(2,1)S(1)} copy-done((bf16[3,384,384]{2,1,0:T(8,128)(2,1)S(1)}, bf16[3,384,384]{2,1,0:T(8,128)(2,1)}, u32[]{:S(2)}) %copy-start) | copy-done | bytes 884760
  1.8 0.0 copy-start.1
  1.8 1.2 %copy-done.1 = bf16[3,384,384]{2,1,0:T(8,128)(2,1)S(1)} copy-done((bf16[3,384,384]{2,1,0:T(8,128)(2,1)S(1)}, bf16[3,384,384]{2,1,0:T(8,128)(2,1)}, u32[]{:S(2)}) %copy-start.1) | copy-done | bytes 884760
  3.0 0.0 copy-start.2
  3.0 0.9 %copy-done.2 = f32[1,1,4,64,216]{4,3,2,1,0:T(8,128)S(1)} copy-done((f32[1,1,4,64,216]{4,3,2,1,0:T(8,128)S(1)}, f32[1,1,4,64,216]{4,3,2,1,0:T(8,128)}, u32[]{:S(2)}) %copy-start.2) | copy-done | bytes 221208
  3.9 0.0 copy-start.4
  3.9 0.9 %copy-done.4 = f32[27,32,16]{1,2,0:T(8,128)S(1)} copy-done((f32[27,32,16]{1,2,0:T(8,128)S(1)}, f32[27,32,16]{1,2,0:T(8,128)}, u32[]{:S(2)}) %copy-start.4) | copy-done | bytes 55320
  4.9 0.0 copy-start.5
  4.9 0.8 %copy-done.5 = f32[27,432]{1,0:T(8,128)S(1)} copy-done((f32[27,432]{1,0:T(8,128)S(1)}, f32[27,432]{1,0:T(8,128)}, u32[]{:S(2)}) %copy-start.5) | copy-done | bytes 46680
  5.7 0.0 copy-start.6
  5.7 0.8 %copy-done.6 = bf16[256,128]{1,0:T(8,128)(2,1)S(1)} copy-done((bf16[256,128]{1,0:T(8,128)(2,1)S(1)}, bf16[256,128]{1,0:T(8,128)(2,1)}, u32[]{:S(2)}) %copy-start.6) | copy-done | bytes 65560
  6.5 0.0 copy-start.7
  6.5 0.8 %copy-done.7 = bf16[256,128]{1,0:T(8,128)(2,1)S(1)} copy-done((bf16[256,128]{1,0:T(8,128)(2,1)S(1)}, bf16[256,128]{1,0:T(8,128)(2,1)}, u32[]{:S(2)}) %copy-start.7) | copy-done | bytes 65560
  7.4 0.0 copy-start.8
  7.4 0.8 %copy-done.8 = f32[27,16,4]{0,2,1:T(4,128)S(1)} copy-done((f32[27,16,4]{0,2,1:T(4,128)S(1)}, f32[27,16,4]{0,2,1:T(4,128)}, u32[]{:S(2)}) %copy-start.8) | copy-done | bytes 6936
  8.1 0.0 copy-start.9
  8.1 0.8 %copy-done.9 = f32[1,1,32,216]{3,2,1,0:T(8,128)S(1)} copy-done((f32[1,1,32,216]{3,2,1,0:T(8,128)S(1)}, f32[1,1,32,216]{3,2,1,0:T(8,128)}, u32[]{:S(2)}) %copy-start.9) | copy-done | bytes 27672
  8.9 30.8 %shard_map.120 = (f32[32,216]{1,0:T(8,128)S(1)}, f32[128,216]{1,0:T(8,128)S(1)}, f32[128,128]{1,0:T(8,128)S(1)}) custom-call(f32[256,216]{1,0:T(8,128)S(1)} %bitcast.22, f32[64,27]{1,0:T(8,128)S(1)} %bitcast.26, f32[432,32]{1,0:T(8,128)S(1)} %bitcast.23, f32[32,216]{1,0:T(8,128)S(1)} %bitcast.27, bf16[3,384,384]{2,1,0:T(8,128)(2,1)S(1)} %copy-done.1, ...), custom_call_target="tpu_custom_call" | custom-call | tf_op jit(solution)/shard_map/pallas_call | solution.py:413
  39.8 24.6 %shard_map.121 = f32[16,8,128]{2,1,0:T(8,128)S(1)} custom-call(f32[16,8,128]{2,1,0:T(8,128)S(1)} %bitcast.25), custom_call_target="tpu_custom_call" | custom-call | tf_op jit(solution)/shard_map/pallas_call | solution.py:447
  64.4 0.0 copy-start.3
  64.4 0.6 copy-done.3
  65.0 0.1 reshape.53
  65.2 0.0 slice-start
  65.2 0.7 %copy.17 = f32[27,16,4]{0,2,1:T(4,128)} copy(f32[27,16,4]{1,0,2:T(8,128)S(1)} %slice_bitcast_fusion.1) | data formatting | bytes 13824
  65.9 0.1 slice-done
  66.0 0.1 reshape.55
  66.2 0.7 %slice_bitcast_fusion = f32[27,32,16]{1,2,0:T(8,128)} fusion(f32[28,16,32]{2,1,0:T(8,128)S(1)} %bitcast.30), kind=kLoop, calls=%fused_computation | loop fusion | bytes 110592 | tf_op jit(solution)/shard_map/transpose | solution.py:477
  66.9 0.6 copy.22
  67.5 0.7 copy.23
  (4 shorter events, 0.0 us)
Async XLA Ops:
  0.6 1.2 %copy-start = (bf16[3,384,384]{2,1,0:T(8,128)(2,1)S(1)}, bf16[3,384,384]{2,1,0:T(8,128)(2,1)}, u32[]{:S(2)}) copy-start(bf16[3,384,384]{2,1,0:T(8,128)(2,1)} %constant.11.clone.high_ref) | copy-start | bytes 2654212
  1.8 1.2 %copy-start.1 = (bf16[3,384,384]{2,1,0:T(8,128)(2,1)S(1)}, bf16[3,384,384]{2,1,0:T(8,128)(2,1)}, u32[]{:S(2)}) copy-start(bf16[3,384,384]{2,1,0:T(8,128)(2,1)} %constant.10.clone.low_ref) | copy-start | bytes 2654212
  3.0 0.9 %copy-start.2 = (f32[1,1,4,64,216]{4,3,2,1,0:T(8,128)S(1)}, f32[1,1,4,64,216]{4,3,2,1,0:T(8,128)}, u32[]{:S(2)}) copy-start(f32[1,1,4,64,216]{4,3,2,1,0:T(8,128)} %param.9) | copy-start | bytes 663556
  3.9 0.9 %copy-start.4 = (f32[27,32,16]{1,2,0:T(8,128)S(1)}, f32[27,32,16]{1,2,0:T(8,128)}, u32[]{:S(2)}) copy-start(f32[27,32,16]{1,2,0:T(8,128)} %param.11) | copy-start | bytes 165892
  4.9 0.8 %copy-start.5 = (f32[27,432]{1,0:T(8,128)S(1)}, f32[27,432]{1,0:T(8,128)}, u32[]{:S(2)}) copy-start(f32[27,432]{1,0:T(8,128)} %constant.14.clone.spread_ref) | copy-start | bytes 139972
  5.7 0.8 %copy-start.6 = (bf16[256,128]{1,0:T(8,128)(2,1)S(1)}, bf16[256,128]{1,0:T(8,128)(2,1)}, u32[]{:S(2)}) copy-start(bf16[256,128]{1,0:T(8,128)(2,1)} %constant.13.clone.pickl_ref) | copy-start | bytes 196612
  6.5 0.8 %copy-start.7 = (bf16[256,128]{1,0:T(8,128)(2,1)S(1)}, bf16[256,128]{1,0:T(8,128)(2,1)}, u32[]{:S(2)}) copy-start(bf16[256,128]{1,0:T(8,128)(2,1)} %constant.12.clone.pick_ref) | copy-start | bytes 196612
  7.4 0.8 %copy-start.8 = (f32[27,16,4]{0,2,1:T(4,128)S(1)}, f32[27,16,4]{0,2,1:T(4,128)}, u32[]{:S(2)}) copy-start(f32[27,16,4]{0,2,1:T(4,128)} %param.10) | copy-start | bytes 20740
  8.1 0.8 %copy-start.9 = (f32[1,1,32,216]{3,2,1,0:T(8,128)S(1)}, f32[1,1,32,216]{3,2,1,0:T(8,128)}, u32[]{:S(2)}) copy-start(f32[1,1,32,216]{3,2,1,0:T(8,128)} %param.12) | copy-start | bytes 82948
  64.4 0.6 copy-start.3
  65.2 0.8 %slice-start = ((f32[16,8,128]{2,1,0:T(8,128)}), f32[14,8,128]{2,1,0:T(8,128)S(1)}, s32[]{:S(2)}) async-start(f32[16,8,128]{2,1,0:T(8,128)} %copy-done.3), calls=%async_computation | async-start | bytes 114688 | tf_op jit(solution)/shard_map/slice | solution.py:469

commit v2 on v1

--- a/solution.py
+++ b/solution.py
@@ -71,6 +71,22 @@
     return m
 
 
+def constant_rows():
+    picks = np.zeros((256, 384), np.float32)
+    picks[:, 0:128] = pick_matrix(SIDE - 1)
+    picks[:, 128:256] = pick_matrix(0)
+    return np.concatenate([*shift_matrices(-1), *shift_matrices(1), picks], axis=0)
+
+
+def collect_matrix():
+    m = np.zeros((432, 128), np.float32)
+    for k in range(27):
+        for c in range(4):
+            m[16 * k + c, 32 * c + k] = 1
+            m[16 * k + 4 + c, 32 * c + k] = 1
+    return m
+
+
 def iota(shape, dim):
     return lax.broadcasted_iota(jnp.int32, shape, dim)
 
@@ -131,11 +147,14 @@
 
 
 def level_kernel(
-    x_ref, w1_ref, w2_ref, g_ref, low_ref, high_ref, pick_ref, pickl_ref, spread_ref,
-    lev_ref, hid_ref, part_ref,
+    x_hbm, w1_hbm, w2_hbm, g_hbm, table_hbm, spread_hbm, collect_hbm,
+    lev_hbm, hid_hbm, one_hbm, two_hbm,
+    x_ref, w1_ref, w2_ref, g_ref, table, spread_ref, collect_ref, load_sem,
+    lev_ref, hid_ref, one_ref, two_ref, store_sem,
     xs, xc, hk, pre, back, send, recv, dsend, drecv, send_sem, recv_sem, dsend_sem, drecv_sem,
+    one_own, one_parts, two_own, two_parts, two_sum, sum_in, sum_out,
 ):
-    where = lax.axis_index("space")
+    dp, where = lax.axis_index("dp"), lax.axis_index("space")
     coords = (where // 16, where // 4 % 4, where % 4)
 
     def neighbour(dims, step):
@@ -152,17 +171,88 @@
             out.append(flag)
         return out
 
+    def load(n, src, dst):
+        copy = pltpu.make_async_copy(src, dst, load_sem.at[n])
+        copy.start()
+        return copy
+
+    load_x = load(0, x_hbm, x_ref)
+    picks, shifts = pl.ds(2304, 256), pl.ds(0, 2304)
+    load_picks = load(1, table_hbm.at[picks], table.at[picks])
+    loads = [
+        load(2, w1_hbm, w1_ref),
+        load(3, spread_hbm, spread_ref),
+        load(4, w2_hbm, w2_ref),
+        load(5, table_hbm.at[shifts], table.at[shifts]),
+        load(6, g_hbm, g_ref),
+        load(7, collect_hbm, collect_ref),
+    ]
+
+    def store(n, src, dst):
+        copy = pltpu.make_async_copy(src, dst, store_sem.at[n])
+        copy.start()
+        return copy
+
+    y, zc = where // 2 % 8, where // 16 * 2 + where % 2
+
+    def on_dp(p):
+        return {"dp": p}
+
+    def on_y(p):
+        return {"space": zc // 2 * 16 + p * 2 + zc % 2}
+
+    def on_zc(p):
+        return {"space": p // 2 * 16 + y * 2 + p % 2}
+
     barrier = pltpu.get_barrier_semaphore()
     for dims in SUBSETS:
         for step in (-1, 1):
             pl.semaphore_signal(barrier, inc=1, device_id=neighbour(dims, step), device_id_type=MESH)
-
+    for me, device in ((dp, on_dp), (y, on_y), (zc, on_zc)):
+        for j in range(1, 8):
+            pl.semaphore_signal(barrier, inc=1, device_id=device((me + j) % 8), device_id_type=MESH)
+
+    def rows16(n):
+        return pl.ds(pl.multiple_of(16 * n, 16), 16)
+
+    sent = []
+
+    def exchange(stage, me, device, src, dst):
+        def copy(j, to):
+            p = (me + j) % 8
+            return pltpu.make_async_remote_copy(
+                src_ref=src(p),
+                dst_ref=dst(to if to is not None else p),
+                send_sem=sum_out.at[stage, j],
+                recv_sem=sum_in.at[stage, to if to is not None else p],
+                device_id=device(p),
+                device_id_type=MESH,
+            )
+
+        for j in range(1, 8):
+            sent.append(copy(j, me))
+            sent[-1].start()
+
+        def wait():
+            for j in range(1, 8):
+                copy(j, None).wait_recv()
+
+        return wait
+
+    def sum_of(parts):
+        parts = [parts[16 * n : 16 * n + 16, :] for n in range(8)]
+        while len(parts) > 1:
+            parts = [parts[n] + parts[n + 1] for n in range(0, len(parts), 2)]
+        return parts[0]
+
+    load_x.wait()
+    load_picks.wait()
+    pick = table[2304:2560, 0:128]
     x = jnp.concatenate([x_ref[...], jnp.zeros((256, 40), F32)], axis=1)
     pieces = split(x, 3)
-    picked = dot(pieces[0], pick_ref[...]) + dot(pieces[1], pick_ref[...])
-    picked = picked + dot(pieces[2], pick_ref[...])
+    picked = dot(pieces[0], pick) + dot(pieces[1], pick) + dot(pieces[2], pick)
     pack([picked[8 * t : 8 * t + 8] for t in range(32)], send, IN_AT)
-    pl.semaphore_wait(barrier, 14)
+    pl.semaphore_wait(barrier, 35)
     copies = []
     for s, dims in enumerate(SUBSETS):
         rows = pl.ds(IN_AT[s], IN_ROWS[s])
@@ -178,6 +268,8 @@
         )
         copies[-1].start()
 
+    for copy in loads:
+        copy.wait()
     w1 = dot(w1_ref[...], spread_ref[...], HIGHEST)
     w1 = jnp.where(iota((64, 432), 0) % 4 == iota((64, 432), 1) % 4, w1, 0.0)
     w1 = dot((iota((16, 64), 1) // 4 == iota((16, 64), 0)).astype(F32), w1, HIGHEST)
@@ -232,7 +324,7 @@
     for d, (ri, rj, rl) in enumerate([((4,), four, four), (five, (4,), four), (five, five, (4,))]):
         source = [cell(i, j, l) for i in ri for j in rj for l in rl]
         target = [at - cell(*[4 if e == d else 0 for e in range(3)]) for at in source]
-        moved = dot(jnp.concatenate([xc[at : at + 16, :] for at in source], axis=0), low_ref[d]).astype(BF16)
+        moved = dot(jnp.concatenate([xc[at : at + 16, :] for at in source], axis=0), table[384 * d : 384 * d + 384, :]).astype(BF16)
         for n, at in enumerate(target):
             xc[at : at + 16, :] = moved[16 * n : 16 * n + 16]
 
@@ -261,7 +353,7 @@
         source = [three((i, j, l)) for i in ri for j in rj for l in rl]
         rows = jnp.concatenate([hk[n, at : at + 16, :] for n in range(3) for at in source], axis=0)
         lanes = 384 if d < 2 else 256
-        moved = dot(rows, low_ref[d, :, 0:lanes]).astype(BF16)
+        moved = dot(rows, table[384 * d : 384 * d + 384, 0:lanes]).astype(BF16)
         step = three([2 if e == d else 0 for e in range(3)])
         for n in range(3):
             for m, at in enumerate(source):
@@ -273,11 +365,12 @@
     r3 = dot(two_lhs[0:32], hk[2, :, 0:256])
     pre_two = ((r[64:96] + r2[32:64]) + r3 + (r[32:64] + r2[0:32])) + r[0:32]
     lev_ref[...] = jnp.where(pre_two > 0, pre_two, SLOPE * pre_two)[:, 0:CELLS]
+    stores = [store(0, lev_ref, lev_hbm)]
     grad = jnp.concatenate([g_ref[...], jnp.zeros((32, 40), F32)], axis=1)
     delta = grad * jnp.where(pre_two > 0, 1.0, SLOPE)
 
     pieces = split(delta, 3)
-    r = dot(jnp.concatenate(pieces, axis=0), pickl_ref[...])
+    r = dot(jnp.concatenate(pieces, axis=0), table[2304:2560, 128:256])
     picked = (r[0:32] + r[32:64]) + r[64:96]
     pack([picked[8 * t : 8 * t + 8] for t in range(4)], dsend, D_AT)
     dcopies = []
@@ -298,7 +391,10 @@
     d1, d2 = pieces[0], pieces[1]
     r = dot_t(hk[0, :, 0:256], d1) + dot_t(hk[0, :, 0:256], d2) + dot_t(hk[1, :, 0:256], d1)
     r = jnp.concatenate([r, jnp.zeros((16, 32), F32)], axis=0)
-    part_ref[0:112, :] = jnp.concatenate([r[112 * n : 112 * n + 112] for n in range(4)], axis=1)
+    two_own[0:112, :] = jnp.concatenate([r[112 * n : 112 * n + 112] for n in range(4)], axis=1)
+    two_own[112:128, :] = jnp.zeros((16, 128), F32)
+    two_parts[0, rows16(dp), :] = two_own[rows16(dp), :]
+    wait_two = exchange(0, dp, on_dp, lambda p: two_own.at[rows16(p)], lambda p: two_parts.at[0, rows16(p)])
 
     for copy in dcopies:
         copy.wait_recv()
@@ -309,117 +405,109 @@
     for d in range(3):
         bit = 4 >> d
         keys = sorted(by_shift)
-        moved = dot(jnp.concatenate([by_shift[s] for s in keys], axis=0), high_ref[d]).astype(BF16)
+        moved = dot(jnp.concatenate([by_shift[s] for s in keys], axis=0), table[1152 + 384 * d : 1536 + 384 * d, :]).astype(BF16)
         for n, s in enumerate(keys):
             by_shift[s | bit] = moved[64 * n : 64 * n + 64]
     da = jnp.concatenate([by_shift[s][0:32, 0:256] for s in range(8)], axis=0)
     db = jnp.concatenate([by_shift[s][32:64, 0:256] for s in range(8)], axis=0)
     r = dot(back_lhs, da)
     r = (r[128:256] + dot(back_lhs[0:128], db)) + r[0:128]
-    total = None
+    ones = []
     for q in range(8):
         value = r[16 * q : 16 * q + 16]
         for t in range(2):
             back[t, pl.ds(q, 16, stride=8), :] = value[:, 128 * t : 128 * t + 128]
-        d_one = value * jnp.where(pre[q] > 0, 1.0, SLOPE)
-        term = dot_t(stacked(q, 256), jnp.concatenate(split(d_one, 2), axis=0))
+        ones.append(jnp.concatenate(split(value * jnp.where(pre[q] > 0, 1.0, SLOPE), 2), axis=0))
+    hid_ref[...] = jnp.concatenate([back[0], back[1]], axis=1)[:, 0:CELLS]
+    stores.append(store(1, hid_ref, hid_hbm))
+
+    def reduce_two(stage, me, device):
+        value = sum_of(two_parts.at[stage - 1])
+        two_sum[stage - 1] = value
+        two_parts[stage, rows16(me), :] = value
+        return exchange(
+            stage, me, device, lambda p: two_sum.at[stage - 1], lambda p: two_parts.at[stage, rows16(p)]
+        )
+
+    wait_two()
+    wait_two = reduce_two(1, y, on_y)
+    total = None
+    for q in range(8):
+        term = dot_t(stacked(q, 256), ones[q])
         total = term if total is None else total + term
-    hid_ref[...] = jnp.concatenate([back[0], back[1]], axis=1)[:, 0:CELLS]
-
-    lane, row = iota((8, 128), 1), iota((8, 128), 0)
-    packed = [jnp.zeros((8, 128), F32), jnp.zeros((8, 128), F32)]
-    for k in range(27):
-        tile = jnp.concatenate([total[16 * k : 16 * k + 8], jnp.zeros((8, 96), F32)], axis=1)
-        tile = tile + pltpu.roll(tile, 112, 1)
-        tile = tile + pltpu.roll(tile, 4, 0)
-        tile = pltpu.roll(tile, 16 * (k % 8), 1)
-        here = (lane // 16 == k % 8) & (row // 4 == k // 8 % 2)
-        packed[k // 16] = jnp.where(here, tile, packed[k // 16])
-    part_ref[112:128, :] = jnp.concatenate(packed, axis=0)
-    for copy in copies + dcopies:
+    small = (iota((16, 32), 1) % 16 == iota((16, 32), 0)).astype(F32)
+    one_own[0] = dot(dot_t(small, total, HIGHEST), collect_ref[...], HIGHEST)
+
+    def reduce_one(stage, me, device):
+        one_parts[stage, rows16(me), :] = one_own[stage]
+        return exchange(
+            4 + stage, me, device, lambda p: one_own.at[stage], lambda p: one_parts.at[stage, rows16(p)]
+        )
+
+    wait_one = reduce_one(0, dp, on_dp)
+    wait_two()
+    wait_two = reduce_two(2, zc, on_zc)
+    wait_one()
+    one_own[1] = sum_of(one_parts.at[0])
+    wait_one = reduce_one(1, y, on_y)
+    wait_two()
+    wait_two = reduce_two(3, dp, on_dp)
+    wait_one()
+    one_own[2] = sum_of(one_parts.at[1])
+    wait_one = reduce_one(2, zc, on_zc)
+    wait_two()
+    for n in range(4):
+        count = 16 * min(7, 27 - 7 * n)
+        two_ref[112 * n : 112 * n + count, :] = two_parts[3, 0:count, 32 * n : 32 * n + 32]
+    stores.append(store(2, two_ref, two_hbm))
+    wait_one()
+    value = sum_of(one_parts.at[2])
+    for c in range(4):
+        one_ref[:, c, :] = value[:, 32 * c : 32 * c + 27]
+    stores.append(store(3, one_ref, one_hbm))
+    for copy in stores:
+        copy.wait()
+    for copy in copies + dcopies + sent:
         copy.wait_send()
 
 
-def sum_kernel(part_ref, out_ref, ra, rb, mine, final, sem_a, sem_b, sem_c, out_a, out_b, out_c):
-    dp, where = lax.axis_index("dp"), lax.axis_index("space")
-    b, core = where // 2, where % 2
-    a = dp * 2 + core
-
-    def near(j):
-        p = (a + j) % 16
-        return p, {"dp": p // 2, "space": b * 2 + p % 2}
-
-    def far(j):
-        p = (b + j) % 32
-        return p, {"space": p * 2 + core}
-
-    barrier = pltpu.get_barrier_semaphore()
-    for j in range(1, 16):
-        pl.semaphore_signal(barrier, inc=1, device_id=near(j)[1], device_id_type=MESH)
-    for j in range(1, 32):
-        pl.semaphore_signal(barrier, inc=1, device_id=far(j)[1], device_id_type=MESH)
-    pl.semaphore_wait(barrier, 46)
-
-    def copy(src, dst, out_sem, in_sem, device):
-        return pltpu.make_async_remote_copy(
-            src_ref=src, dst_ref=dst, send_sem=out_sem, recv_sem=in_sem, device_id=device, device_id_type=MESH
-        )
-
-    first = []
-    for j in range(1, 16):
-        p, device = near(j)
-        first.append(copy(part_ref.at[p], ra.at[a], out_a.at[j], sem_a.at[a], device))
-        first[-1].start()
-    ra[a] = part_ref[a]
-    for j in range(1, 16):
-        p, device = near(j)
-        copy(part_ref.at[p], ra.at[p], out_a.at[j], sem_a.at[p], device).wait_recv()
-    value = jnp.sum(ra[...], axis=0)
-    mine[...] = value
-    rb[b] = value
-    second = []
-    for j in range(1, 32):
-        p, device = far(j)
-        second.append(copy(mine, rb.at[b], out_b.at[j], sem_b.at[b], device))
-        second[-1].start()
-    for j in range(1, 32):
-        p, device = far(j)
-        copy(mine, rb.at[p], out_b.at[j], sem_b.at[p], device).wait_recv()
-    value = jnp.sum(rb[...], axis=0)
-    final[...] = value
-    out_ref[a] = value
-    third = []
-    for j in range(1, 16):
-        p, device = near(j)
-        third.append(copy(final, out_ref.at[a], out_c.at[j], sem_c.at[a], device))
-        third[-1].start()
-    for j in range(1, 16):
-        p, device = near(j)
-        copy(final, out_ref.at[p], out_c.at[j], sem_c.at[p], device).wait_recv()
-    for c in first + second + third:
-        c.wait_send()
+def finish_kernel(*refs):
+    sem = refs[-1]
+    copies = [pltpu.make_async_copy(refs[n], refs[4 + n], sem.at[n]) for n in range(4)]
+    for copy in copies:
+        copy.start()
+    for copy in copies:
+        copy.wait()
 
 
 def body(volume_in, filter_one, filter_two, out_grad):
-    vmem = pl.BlockSpec(memory_space=pltpu.VMEM)
+    hbm = pl.BlockSpec(memory_space=pltpu.HBM)
     dma = pltpu.SemaphoreType.DMA
-    constants = [
-        jnp.asarray(shift_matrices(-1), BF16),
-        jnp.asarray(shift_matrices(1), BF16),
-        jnp.asarray(pick_matrix(SIDE - 1), BF16),
-        jnp.asarray(pick_matrix(0), BF16),
-        jnp.asarray(spread_matrix(), F32),
+    shapes = [
+        jax.ShapeDtypeStruct((32, CELLS), F32),
+        jax.ShapeDtypeStruct((128, CELLS), F32),
+        jax.ShapeDtypeStruct((16, 4, 27), F32),
+        jax.ShapeDtypeStruct((432, 32), F32),
     ]
-    level, hidden, part = pl.pallas_call(
+    results = pl.pallas_call(
         level_kernel,
-        out_shape=[
-            jax.ShapeDtypeStruct((32, CELLS), F32),
-            jax.ShapeDtypeStruct((128, CELLS), F32),
-            jax.ShapeDtypeStruct((128, 128), F32),
-        ],
-        in_specs=[vmem] * 9,
-        out_specs=[vmem] * 3,
+        out_shape=shapes,
+        in_specs=[hbm] * 7,
+        out_specs=[hbm] * 4,
         scratch_shapes=[
+            pltpu.VMEM((256, CELLS), F32),
+            pltpu.VMEM((64, 27), F32),
+            pltpu.VMEM((432, 32), F32),
+            pltpu.VMEM((32, CELLS), F32),
+            pltpu.VMEM((2560, 384), BF16),
+            pltpu.VMEM((27, 432), F32),
+            pltpu.VMEM((432, 128), F32),
+            dma((8,)),
+            pltpu.VMEM((32, CELLS), F32),
+            pltpu.VMEM((128, CELLS), F32),
+            pltpu.VMEM((16, 4, 27), F32),
+            pltpu.VMEM((432, 32), F32),
+            dma((4,)),
             pltpu.VMEM((3, 512, 128), F32),
             pltpu.VMEM((2000, 384), BF16),
             pltpu.VMEM((3, 432, 384), BF16),
@@ -433,48 +521,39 @@
             dma((7,)),
             dma((7,)),
             dma((7,)),
+            pltpu.VMEM((3, 16, 128), F32),
+            pltpu.VMEM((3, 128, 128), F32),
+            pltpu.VMEM((128, 128), F32),
+            pltpu.VMEM((4, 128, 128), F32),
+            pltpu.VMEM((3, 16, 128), F32),
+            dma((7, 8)),
+            dma((7, 8)),
         ],
         compiler_params=pltpu.CompilerParams(
-            collective_id=0, has_side_effects=True, vmem_limit_bytes=48 * 2**20
+            collective_id=0, has_side_effects=True, vmem_limit_bytes=60 * 2**20
         ),
     )(
         volume_in.reshape(256, CELLS),
         jnp.transpose(filter_one, (1, 2, 0)).reshape(64, 27),
         jnp.transpose(filter_two, (0, 2, 1)).reshape(432, 32),
         out_grad.reshape(32, CELLS),
-        *constants,
+        jnp.asarray(constant_rows(), BF16),
+        jnp.asarray(spread_matrix(), F32),
+        jnp.asarray(collect_matrix(), F32),
     )
-    total = pl.pallas_call(
-        sum_kernel,
-        out_shape=jax.ShapeDtypeStruct((16, 8, 128), F32),
-        in_specs=[vmem],
-        out_specs=vmem,
-        scratch_shapes=[
-            pltpu.VMEM((16, 8, 128), F32),
-            pltpu.VMEM((32, 8, 128), F32),
-            pltpu.VMEM((8, 128), F32),
-            pltpu.VMEM((8, 128), F32),
-            dma((16,)),
-            dma((32,)),
-            dma((16,)),
-            dma((16,)),
-            dma((32,)),
-            dma((16,)),
-        ],
-        compiler_params=pltpu.CompilerParams(
-            collective_id=1, has_side_effects=True, vmem_limit_bytes=16 * 2**20
-        ),
-    )(part.reshape(16, 8, 128))
-    total = total.reshape(128, 128)
-    grad_two = total[0:112].reshape(7, 16, 4, 32)
-    grad_two = jnp.transpose(grad_two, (2, 0, 1, 3)).reshape(28, 16, 32)[0:27]
-    grad_one = total[112:128].reshape(4, 4, 8, 16)
-    grad_one = jnp.transpose(grad_one, (0, 2, 1, 3)).reshape(32, 4, 16)[0:27]
+    level, hidden, grad_one, grad_two = pl.pallas_call(
+        finish_kernel,
+        out_shape=shapes,
+        in_specs=[hbm] * 4,
+        out_specs=[hbm] * 4,
+        scratch_shapes=[dma((4,))],
+        compiler_params=pltpu.CompilerParams(vmem_limit_bytes=60 * 2**20),
+    )(*results)
     return (
         level.reshape(1, 1, 32, CELLS),
         hidden.reshape(1, 1, 16, 8, CELLS),
-        jnp.transpose(grad_one, (0, 2, 1)),
-        jnp.transpose(grad_two, (0, 2, 1)),
+        jnp.transpose(grad_one, (2, 0, 1)),
+        jnp.transpose(grad_two.reshape(27, 16, 32), (0, 2, 1)),
     )
 
 

time: 68.7 us -> 62.8 us (0.914)
  local copies, waits for them, and re-layouts: 11.9 us -> 0 us
  Pallas kernels: 55.5 us -> 62 us
    unnamed x23 -> x0, local copies, waits for them, and re-layouts: 10.8 us -> none
    pallas_call x2, Pallas kernels: 55.5 us -> 62 us  [the longest x1 48.2 us: body(): pl.pallas_call(level_kernel, out_shape=shapes, in_specs=[hbm] * 7, out_sp...]
    transpose x3 -> x0, local copies, waits for them, and re-layouts: 0.72 us -> none  [the longest x1 0.7 us: body(): jnp.transpose(grad_two, (0, 2, 1))]
where the time goes in v2:
time: 62.8 us; the launch traced here: 62.6 us
  Pallas kernels  62 us (99%)
  between operations  0.64 us (1%)
    pallas_call x1, Pallas kernels, body(): pl.pallas_call(level_kernel, out_shape=shapes, in_specs=[hbm] * 7, out_sp...  48.2 us
    pallas_call x1, Pallas kernels, body(): pl.pallas_call(finish_kernel, out_shape=shapes, in_specs=[hbm] * 4, out_s...  13.8 us

profile of v2, /device:TPU:1, one launch (start us, length us, event | category | flops | bytes accessed | tf_op | source)
XLA Modules:
  0.0 62.6 jit_solution(17981044470913489536)
XLA Ops:
  0.6 48.2 %shard_map.102 = (f32[32,216]{1,0:T(8,128)}, f32[128,216]{1,0:T(8,128)}, f32[16,4,27]{2,1,0:T(4,128)}, f32[432,32]{1,0:T(8,128)}) custom-call(f32[256,216]{1,0:T(8,128)} %bitcast.14, f32[64,27]{1,0:T(8,128)} %bitcast.16, f32[432,32]{1,0:T(8,128)} %bitcast.15, f32[32,216]{1,0:T(8,128)} %bitcast.17, bf16[2560,384]{1,0:T(8,128)(2,1)} %constant.6.clone.table_hbm, ...), custom_call_target="tpu_custom_call" | custom-call | tf_op jit(solution)/shard_map/pallas_call | solution.py:492
  48.8 13.8 %shard_map.103 = (f32[32,216]{1,0:T(8,128)}, f32[128,216]{1,0:T(8,128)}, f32[16,4,27]{2,1,0:T(4,128)}, f32[432,32]{1,0:T(8,128)}) custom-call(f32[32,216]{1,0:T(8,128)} %get-tuple-element.12.refs_0_, f32[128,216]{1,0:T(8,128)} %get-tuple-element.13.refs_1_, f32[16,4,27]{2,1,0:T(4,128)} %get-tuple-element.14.refs_2_, f32[432,32]{1,0:T(8,128)} %get-tuple-element.15.refs_3_), custom_call_target="tpu_custom_call" | custom-call | tf_op jit(solution)/shard_map/pallas_call | solution.py:544

commit v3 on v2

--- a/solution.py
+++ b/solution.py
@@ -21,13 +21,13 @@
 STARTS = [sum(SIZES[:i]) for i in range(7)]
 
 
-def rows_for(tiles):
-    rows = [8 * -(-tiles // (128 // size)) for size in SIZES]
+def rows_for(counts):
+    rows = [8 * -(-tiles // (128 // size)) for tiles, size in zip(counts, SIZES)]
     return rows, [sum(rows[:i]) for i in range(7)]
 
 
-IN_ROWS, IN_AT = rows_for(32)
-D_ROWS, D_AT = rows_for(4)
+IN_ROWS, IN_AT = rows_for([24, 24, 24, 32, 32, 32, 32])
+D_ROWS, D_AT = rows_for([4] * 7)
 
 
 def lane_of(coords, outside):
@@ -42,13 +42,12 @@
 def shift_matrices(step):
     outside = -1 if step < 0 else SIDE
     span = range(-1, SIDE) if step < 0 else range(SIDE + 1)
-    m = np.zeros((3, 384, 384), np.float32)
+    m = np.zeros((7, 384, 384), np.float32)
     for coords in itertools.product(span, repeat=3):
-        for d in range(3):
-            source = list(coords)
-            source[d] += step
-            if coords[d] != outside:
-                m[d, lane_of(source, outside), lane_of(coords, outside)] = 1
+        for s, dims in enumerate(SUBSETS):
+            source = [c + (step if d in dims else 0) for d, c in enumerate(coords)]
+            if all(coords[d] != outside for d in dims):
+                m[s, lane_of(source, outside), lane_of(coords, outside)] = 1
     return m
 
 
@@ -75,7 +74,7 @@
     picks = np.zeros((256, 384), np.float32)
     picks[:, 0:128] = pick_matrix(SIDE - 1)
     picks[:, 128:256] = pick_matrix(0)
-    return np.concatenate([*shift_matrices(-1), *shift_matrices(1), picks], axis=0)
+    return np.concatenate([picks, *shift_matrices(-1), *shift_matrices(1)], axis=0)
 
 
 def collect_matrix():
@@ -108,27 +107,50 @@
     return lax.dot_general(a, b, (((1,), (1,)), ((), ())), preferred_element_type=F32, precision=precision)
 
 
-def pack(tiles, buf, starts):
+def trimmed(tiles, d):
+    weight = 4 >> d
+    own = (iota((8, 128), 0) // weight) % 2 == 1
+    other = 4 >> (d + 1) % 3
+    out = []
+    for t, tile in enumerate(tiles):
+        if t & weight:
+            out.append(tile)
+        elif not t & other:
+            out.append(jnp.where(own, tile, pltpu.roll(tiles[t | other], 8 - weight, 0)))
+    return out
+
+
+def trimmed_place(t, d):
+    weight, other = 4 >> d, 4 >> (d + 1) % 3
+    places = [n for n in range(32) if n & weight or not n & other]
+    return (places.index(t), False) if t & weight else (places.index(t & ~other), bool(t & other))
+
+
+def pack(tiles, buf, starts, trim=False):
     lane = iota((8, 128), 1)
     for s in range(7):
         size = SIZES[s]
         per = 128 // size
-        for block in range(-(-len(tiles) // per)):
+        these = trimmed(tiles, s) if trim and s < 3 else tiles
+        for block in range(-(-len(these) // per)):
             total = jnp.zeros((8, 128), F32)
-            for i, tile in enumerate(tiles[block * per : (block + 1) * per]):
+            for i, tile in enumerate(these[block * per : (block + 1) * per]):
                 moved = pltpu.roll(tile, (i * size - STARTS[s]) % 128, 1)
                 total = jnp.where((lane >= i * size) & (lane < (i + 1) * size), moved, total)
             buf[starts[s] + 8 * block : starts[s] + 8 * block + 8, :] = total
 
 
-def unpack(t, buf, starts, valid):
+def unpack(t, buf, starts, valid, trim=False):
     lane = iota((8, 128), 1)
     total = jnp.zeros((8, 128), F32)
     for s in range(7):
         size = SIZES[s]
         per = 128 // size
-        row = starts[s] + 8 * (t // per)
-        moved = pltpu.roll(buf[row : row + 8, :], (STARTS[s] - (t % per) * size) % 128, 1)
+        n, second = trimmed_place(t, s) if trim and s < 3 else (t, False)
+        row = starts[s] + 8 * (n // per)
+        moved = pltpu.roll(buf[row : row + 8, :], (STARTS[s] - (n % per) * size) % 128, 1)
+        if second:
+            moved = pltpu.roll(moved, 4 >> s, 0)
         here = (lane >= STARTS[s]) & (lane < STARTS[s] + size) & (valid[s] > 0)
         total = jnp.where(here, moved, total)
     return total
@@ -155,10 +177,21 @@
     one_own, one_parts, two_own, two_parts, two_sum, sum_in, sum_out,
 ):
     dp, where = lax.axis_index("dp"), lax.axis_index("space")
-    coords = (where // 16, where // 4 % 4, where % 4)
+    gx = lax.div(where, 16)
+    rest = where - 16 * gx
+    gy = lax.div(rest, 4)
+    coords = (gx, gy, rest - 4 * gy)
+    y = lax.div(rest, 2)
+    core = rest - 2 * y
+
+    def wrap(value, size):
+        return jnp.where(value >= size, value - size, value)
+
+    ups = [wrap(c + 1, 4) for c in coords]
+    downs = [wrap(c + 3, 4) for c in coords]
 
     def neighbour(dims, step):
-        moved = [(coords[d] + (step if d in dims else 0) + 4) % 4 for d in range(3)]
+        moved = [(ups if step > 0 else downs)[d] if d in dims else coords[d] for d in range(3)]
         return {"space": moved[0] * 16 + moved[1] * 4 + moved[2]}
 
     def flags(edge):
@@ -177,7 +210,7 @@
         return copy
 
     load_x = load(0, x_hbm, x_ref)
-    picks, shifts = pl.ds(2304, 256), pl.ds(0, 2304)
+    picks, shifts = pl.ds(0, 256), pl.ds(256, 5376)
     load_picks = load(1, table_hbm.at[picks], table.at[picks])
     loads = [
         load(2, w1_hbm, w1_ref),
@@ -193,49 +226,53 @@
         copy.start()
         return copy
 
-    y, zc = where // 2 % 8, where // 16 * 2 + where % 2
-
-    def on_dp(p):
-        return {"dp": p}
-
-    def on_y(p):
-        return {"space": zc // 2 * 16 + p * 2 + zc % 2}
-
-    def on_zc(p):
-        return {"space": p // 2 * 16 + y * 2 + p % 2}
+    z_lo = lax.div(dp, 4)
+    x_at, z_at = dp - 4 * z_lo, 2 * gx + z_lo
+    xc_at = 2 * x_at + core
+    xc_peers = []
+    for j in range(4):
+        p = wrap(x_at + j, 4)
+        for c in (core, 1 - core):
+            xc_peers.append((2 * p + c, {"dp": 4 * z_lo + p, "space": 16 * gx + 2 * y + c}))
+    xc_peers = xc_peers[1:]
+    y_peers = [(p, {"space": 16 * gx + 2 * p + core}) for p in (wrap(y + j, 8) for j in range(1, 8))]
+    z_peers = []
+    for j in range(1, 8):
+        p = wrap(z_at + j, 8)
+        high = lax.div(p, 2)
+        z_peers.append((p, {"dp": 4 * (p - 2 * high) + x_at, "space": 16 * high + 2 * y + core}))
 
     barrier = pltpu.get_barrier_semaphore()
     for dims in SUBSETS:
         for step in (-1, 1):
             pl.semaphore_signal(barrier, inc=1, device_id=neighbour(dims, step), device_id_type=MESH)
-    for me, device in ((dp, on_dp), (y, on_y), (zc, on_zc)):
-        for j in range(1, 8):
-            pl.semaphore_signal(barrier, inc=1, device_id=device((me + j) % 8), device_id_type=MESH)
+    for _, device in xc_peers + z_peers:
+        pl.semaphore_signal(barrier, inc=1, device_id=device, device_id_type=MESH)
 
     def rows16(n):
         return pl.ds(pl.multiple_of(16 * n, 16), 16)
 
     sent = []
 
-    def exchange(stage, me, device, src, dst):
+    def exchange(stage, me, peers, src, dst):
         def copy(j, to):
-            p = (me + j) % 8
+            p, device = peers[j]
             return pltpu.make_async_remote_copy(
                 src_ref=src(p),
-                dst_ref=dst(to if to is not None else p),
+                dst_ref=dst(to),
                 send_sem=sum_out.at[stage, j],
-                recv_sem=sum_in.at[stage, to if to is not None else p],
-                device_id=device(p),
+                recv_sem=sum_in.at[stage, to],
+                device_id=device,
                 device_id_type=MESH,
             )
 
-        for j in range(1, 8):
+        for j in range(7):
             sent.append(copy(j, me))
             sent[-1].start()
 
         def wait():
-            for j in range(1, 8):
-                copy(j, None).wait_recv()
+            for j in range(7):
+                copy(j, peers[j][0]).wait_recv()
 
         return wait
 
@@ -247,12 +284,12 @@
 
     load_x.wait()
     load_picks.wait()
-    pick = table[2304:2560, 0:128]
+    pick = table[0:256, 0:128]
     x = jnp.concatenate([x_ref[...], jnp.zeros((256, 40), F32)], axis=1)
     pieces = split(x, 3)
     picked = dot(pieces[0], pick) + dot(pieces[1], pick) + dot(pieces[2], pick)
-    pack([picked[8 * t : 8 * t + 8] for t in range(32)], send, IN_AT)
-    pl.semaphore_wait(barrier, 35)
+    pack([picked[8 * t : 8 * t + 8] for t in range(32)], send, IN_AT, True)
+    pl.semaphore_wait(barrier, 28)
     copies = []
     for s, dims in enumerate(SUBSETS):
         rows = pl.ds(IN_AT[s], IN_ROWS[s])
@@ -268,7 +305,7 @@
         )
         copies[-1].start()
 
-    for copy in loads:
+    for copy in loads[0:3]:
         copy.wait()
     w1 = dot(w1_ref[...], spread_ref[...], HIGHEST)
     w1 = jnp.where(iota((64, 432), 0) % 4 == iota((64, 432), 1) % 4, w1, 0.0)
@@ -276,7 +313,10 @@
     slot = iota((16, 432), 1) // 4 % 4
     zero = jnp.zeros((16, 432), BF16)
     w1a, w1b, w1c = split(w1, 3)
-    one_lhs = jnp.concatenate([w1a, jnp.where(slot < 2, w1b, zero), jnp.where(slot < 1, w1c, zero)], axis=0)
+    large = jnp.where(slot == 0, w1a, zero)
+    middle = jnp.where(slot == 0, w1b, jnp.where(slot == 1, w1a, zero))
+    least = jnp.where(slot == 0, w1c, jnp.where(slot == 1, w1b, jnp.where(slot == 2, w1a, zero)))
+    one_lhs = jnp.concatenate([large, middle, least], axis=0)
     eye = (iota((32, 32), 0) == iota((32, 32), 1)).astype(F32)
     two_lhs = jnp.concatenate(split(dot_t(eye, w2_ref[...], HIGHEST), 3), axis=0)
     back_rows = []
@@ -311,22 +351,39 @@
 
     gather(0)
     gather(1)
+    def down(s, first, last, lanes):
+        return table[256 + 384 * s + first : 256 + 384 * s + last, 0:lanes]
+
+    def up(s, first, last):
+        return table[2944 + 384 * s + first : 2944 + 384 * s + last, 0:256]
+
+    def shifted_cells(s):
+        places = itertools.product(*[(4,) if d in SUBSETS[s] else range(1, 5) for d in range(3)])
+        source = [cell(*place) for place in places]
+        step = cell(*[4 if d in SUBSETS[s] else 0 for d in range(3)])
+        return source, [at - step for at in source]
+
+    for copy in loads[3:]:
+        copy.wait()
+    for s in range(7):
+        source, target = shifted_cells(s)
+        moved = dot(jnp.concatenate([xc[at : at + 16, 0:256] for at in source], axis=0), down(s, 0, 256, 256)).astype(BF16)
+        for n, at in enumerate(target):
+            xc[at : at + 16, 0:256] = moved[16 * n : 16 * n + 16]
     for copy in copies:
         copy.wait_recv()
     lower = flags(0)
     for t in range(32):
-        tile = unpack(t, recv, IN_AT, lower)
+        tile = unpack(t, recv, IN_AT, lower, True)
         xs[2, 8 * t : 8 * t + 8] = tile
         xs[2, 256 + 8 * t : 264 + 8 * t] = tile
     gather(2)
-
-    four, five = range(1, 5), range(5)
-    for d, (ri, rj, rl) in enumerate([((4,), four, four), (five, (4,), four), (five, five, (4,))]):
-        source = [cell(i, j, l) for i in ri for j in rj for l in rl]
-        target = [at - cell(*[4 if e == d else 0 for e in range(3)]) for at in source]
-        moved = dot(jnp.concatenate([xc[at : at + 16, :] for at in source], axis=0), table[384 * d : 384 * d + 384, :]).astype(BF16)
+    for s in range(7):
+        source, target = shifted_cells(s)
+        moved = dot(jnp.concatenate([xc[at : at + 16, 256:384] for at in source], axis=0), down(s, 256, 384, 384)).astype(BF16)
         for n, at in enumerate(target):
-            xc[at : at + 16, :] = moved[16 * n : 16 * n + 16]
+            xc[at : at + 16, 0:256] += moved[16 * n : 16 * n + 16, 0:256]
+            xc[at : at + 16, 256:384] = moved[16 * n : 16 * n + 16, 256:384]
 
     def stacked(q, lanes):
         b = bits(q)
@@ -348,19 +405,19 @@
         for n, piece in enumerate(split(hidden, 3)):
             hk[n, at : at + 16, :] = piece
 
-    two = range(1, 3)
-    for d, (ri, rj, rl) in enumerate([((2,), two, two), (range(3), (2,), two), (range(3), range(3), (2,))]):
-        source = [three((i, j, l)) for i in ri for j in rj for l in rl]
+    for s, dims in enumerate(SUBSETS):
+        places = itertools.product(*[(2,) if d in dims else (1, 2) for d in range(3)])
+        source = [three(place) for place in places]
         rows = jnp.concatenate([hk[n, at : at + 16, :] for n in range(3) for at in source], axis=0)
-        lanes = 384 if d < 2 else 256
-        moved = dot(rows, table[384 * d : 384 * d + 384, 0:lanes]).astype(BF16)
-        step = three([2 if e == d else 0 for e in range(3)])
+        moved = dot(rows, down(s, 0, 384, 256)).astype(BF16)
+        step = three([2 if d in dims else 0 for d in range(3)])
         for n in range(3):
             for m, at in enumerate(source):
                 row = 16 * (n * len(source) + m)
-                hk[n, at - step : at - step + 16, 0:lanes] = moved[row : row + 16]
-
-    r = dot(two_lhs, hk[0, :, 0:256])
+                hk[n, at - step : at - step + 16, 0:256] = moved[row : row + 16]
+
+    r = [dot(two_lhs[:, 144 * n : 144 * n + 144], hk[0, 144 * n : 144 * n + 144, 0:256]) for n in range(3)]
+    r = (r[0] + r[1]) + r[2]
     r2 = dot(two_lhs[0:64], hk[1, :, 0:256])
     r3 = dot(two_lhs[0:32], hk[2, :, 0:256])
     pre_two = ((r[64:96] + r2[32:64]) + r3 + (r[32:64] + r2[0:32])) + r[0:32]
@@ -370,7 +427,7 @@
     delta = grad * jnp.where(pre_two > 0, 1.0, SLOPE)
 
     pieces = split(delta, 3)
-    r = dot(jnp.concatenate(pieces, axis=0), table[2304:2560, 128:256])
+    r = dot(jnp.concatenate(pieces, axis=0), table[0:256, 128:256])
     picked = (r[0:32] + r[32:64]) + r[64:96]
     pack([picked[8 * t : 8 * t + 8] for t in range(4)], dsend, D_AT)
     dcopies = []
@@ -393,23 +450,23 @@
     r = jnp.concatenate([r, jnp.zeros((16, 32), F32)], axis=0)
     two_own[0:112, :] = jnp.concatenate([r[112 * n : 112 * n + 112] for n in range(4)], axis=1)
     two_own[112:128, :] = jnp.zeros((16, 128), F32)
-    two_parts[0, rows16(dp), :] = two_own[rows16(dp), :]
-    wait_two = exchange(0, dp, on_dp, lambda p: two_own.at[rows16(p)], lambda p: two_parts.at[0, rows16(p)])
-
+    two_parts[0, rows16(xc_at), :] = two_own[rows16(xc_at), :]
+    wait_two = exchange(0, xc_at, xc_peers, lambda p: two_own.at[rows16(p)], lambda p: two_parts.at[0, rows16(p)])
+
+    own = jnp.concatenate([d1, d2], axis=0)
+    moved = [own] * 8
+    for s, dims in enumerate(SUBSETS):
+        moved[sum(4 >> d for d in dims)] = dot(own, up(s, 0, 256)).astype(BF16)
     for copy in dcopies:
         copy.wait_recv()
     higher = flags(3)
     halo = jnp.concatenate([unpack(t, drecv, D_AT, higher) for t in range(4)], axis=0)
-    both = jnp.concatenate(split(jnp.concatenate([delta, halo], axis=1), 2), axis=0)
-    by_shift = {0: both}
-    for d in range(3):
-        bit = 4 >> d
-        keys = sorted(by_shift)
-        moved = dot(jnp.concatenate([by_shift[s] for s in keys], axis=0), table[1152 + 384 * d : 1536 + 384 * d, :]).astype(BF16)
-        for n, s in enumerate(keys):
-            by_shift[s | bit] = moved[64 * n : 64 * n + 64]
-    da = jnp.concatenate([by_shift[s][0:32, 0:256] for s in range(8)], axis=0)
-    db = jnp.concatenate([by_shift[s][32:64, 0:256] for s in range(8)], axis=0)
+    halo = jnp.concatenate(split(halo, 2), axis=0)
+    for s, dims in enumerate(SUBSETS):
+        n = sum(4 >> d for d in dims)
+        moved[n] += dot(halo, up(s, 256, 384)).astype(BF16)
+    da = jnp.concatenate([m[0:32] for m in moved], axis=0)
+    db = jnp.concatenate([m[32:64] for m in moved], axis=0)
     r = dot(back_lhs, da)
     r = (r[128:256] + dot(back_lhs[0:128], db)) + r[0:128]
     ones = []
@@ -430,7 +487,7 @@
         )
 
     wait_two()
-    wait_two = reduce_two(1, y, on_y)
+    wait_two = reduce_two(1, y, y_peers)
     total = None
     for q in range(8):
         term = dot_t(stacked(q, 256), ones[q])
@@ -444,17 +501,17 @@
             4 + stage, me, device, lambda p: one_own.at[stage], lambda p: one_parts.at[stage, rows16(p)]
         )
 
-    wait_one = reduce_one(0, dp, on_dp)
+    wait_one = reduce_one(0, xc_at, xc_peers)
     wait_two()
-    wait_two = reduce_two(2, zc, on_zc)
+    wait_two = reduce_two(2, z_at, z_peers)
     wait_one()
     one_own[1] = sum_of(one_parts.at[0])
-    wait_one = reduce_one(1, y, on_y)
+    wait_one = reduce_one(1, y, y_peers)
     wait_two()
-    wait_two = reduce_two(3, dp, on_dp)
+    wait_two = reduce_two(3, xc_at, xc_peers)
     wait_one()
     one_own[2] = sum_of(one_parts.at[1])
-    wait_one = reduce_one(2, zc, on_zc)
+    wait_one = reduce_one(2, z_at, z_peers)
     wait_two()
     for n in range(4):
         count = 16 * min(7, 27 - 7 * n)
@@ -472,11 +529,15 @@
 
 
 def finish_kernel(*refs):
-    sem = refs[-1]
-    copies = [pltpu.make_async_copy(refs[n], refs[4 + n], sem.at[n]) for n in range(4)]
-    for copy in copies:
+    in_sem, out_sem = refs[-2:]
+    loads = [pltpu.make_async_copy(refs[n], refs[8 + n], in_sem.at[n]) for n in range(4)]
+    stores = [pltpu.make_async_copy(refs[8 + n], refs[4 + n], out_sem.at[n]) for n in range(4)]
+    for copy in loads:
         copy.start()
-    for copy in copies:
+    for load, copy in zip(loads, stores):
+        load.wait()
+        copy.start()
+    for copy in stores:
         copy.wait()
 
 
@@ -499,7 +560,7 @@
             pltpu.VMEM((64, 27), F32),
             pltpu.VMEM((432, 32), F32),
             pltpu.VMEM((32, CELLS), F32),
-            pltpu.VMEM((2560, 384), BF16),
+            pltpu.VMEM((5632, 384), BF16),
             pltpu.VMEM((27, 432), F32),
             pltpu.VMEM((432, 128), F32),
             dma((8,)),
@@ -546,7 +607,7 @@
         out_shape=shapes,
         in_specs=[hbm] * 4,
         out_specs=[hbm] * 4,
-        scratch_shapes=[dma((4,))],
+        scratch_shapes=[*(pltpu.VMEM(shape.shape, F32) for shape in shapes), dma((4,)), dma((4,))],
         compiler_params=pltpu.CompilerParams(vmem_limit_bytes=60 * 2**20),
     )(*results)
     return (

time: 62.8 us -> 48.1 us (0.77)
  Pallas kernels: 62 us -> 47.3 us
    pallas_call x1, Pallas kernels: 13.8 us -> 1.79 us  [body(): pl.pallas_call(finish_kernel, out_shape=shapes, in_specs=[hbm] * 4, out_s...]
    pallas_call x1, Pallas kernels: 48.2 us -> 45.5 us  [body(): pl.pallas_call(level_kernel, out_shape=shapes, in_specs=[hbm] * 7, out_sp...]
where the time goes in v3:
time: 48.1 us; the launch traced here: 47.9 us
  Pallas kernels  47.3 us (98%)
  between operations  0.64 us (1%)
    pallas_call x1, Pallas kernels, body(): pl.pallas_call(level_kernel, out_shape=shapes, in_specs=[hbm] * 7, out_sp...  45.5 us
    pallas_call x1, Pallas kernels, body(): pl.pallas_call(finish_kernel, out_shape=shapes, in_specs=[hbm] * 4, out_s...  1.79 us

profile of v3, /device:TPU:1, one launch (start us, length us, event | category | flops | bytes accessed | tf_op | source)
XLA Modules:
  0.0 47.9 jit_solution(5077381774007718833)
XLA Ops:
  0.6 45.5 %shard_map.102 = (f32[32,216]{1,0:T(8,128)}, f32[128,216]{1,0:T(8,128)}, f32[16,4,27]{2,1,0:T(4,128)}, f32[432,32]{1,0:T(8,128)}) custom-call(f32[256,216]{1,0:T(8,128)} %bitcast.14, f32[64,27]{1,0:T(8,128)} %bitcast.16, f32[432,32]{1,0:T(8,128)} %bitcast.15, f32[32,216]{1,0:T(8,128)} %bitcast.17, bf16[5632,384]{1,0:T(8,128)(2,1)} %constant.6.clone.table_hbm, ...), custom_call_target="tpu_custom_call" | custom-call | tf_op jit(solution)/shard_map/pallas_call | solution.py:553
  46.1 1.8 %shard_map.103 = (f32[32,216]{1,0:T(8,128)}, f32[128,216]{1,0:T(8,128)}, f32[16,4,27]{2,1,0:T(4,128)}, f32[432,32]{1,0:T(8,128)}) custom-call(f32[32,216]{1,0:T(8,128)} %get-tuple-element.12.refs_0_, f32[128,216]{1,0:T(8,128)} %get-tuple-element.13.refs_1_, f32[16,4,27]{2,1,0:T(4,128)} %get-tuple-element.14.refs_2_, f32[432,32]{1,0:T(8,128)} %get-tuple-element.15.refs_3_), custom_call_target="tpu_custom_call" | custom-call | tf_op jit(solution)/shard_map/pallas_call | solution.py:605

commit v4 on v3

--- a/solution.py
+++ b/solution.py
@@ -39,15 +39,23 @@
     return place if not dims else 256 + STARTS[SUBSETS.index(dims)] + place
 
 
-def shift_matrices(step):
-    outside = -1 if step < 0 else SIDE
-    span = range(-1, SIDE) if step < 0 else range(SIDE + 1)
+def down_matrices():
     m = np.zeros((7, 384, 384), np.float32)
-    for coords in itertools.product(span, repeat=3):
+    for coords in itertools.product(range(-1, SIDE), repeat=3):
         for s, dims in enumerate(SUBSETS):
-            source = [c + (step if d in dims else 0) for d, c in enumerate(coords)]
-            if all(coords[d] != outside for d in dims):
-                m[s, lane_of(source, outside), lane_of(coords, outside)] = 1
+            source = [c - (d in dims) for d, c in enumerate(coords)]
+            if all(coords[d] != -1 for d in dims):
+                m[s, lane_of(source, -1), lane_of(coords, -1)] = 1
+    return m
+
+
+def up_matrices():
+    m = np.zeros((7, 384, 384), np.float32)
+    for coords in itertools.product(range(-1, SIDE), repeat=3):
+        for s, dims in enumerate(SUBSETS):
+            source = [c + (d in dims) for d, c in enumerate(coords)]
+            if min(source) >= 0 and (min(coords) >= 0 or max(source) < SIDE):
+                m[s, lane_of(source, SIDE), lane_of(coords, -1)] = 1
     return m
 
 
@@ -74,7 +82,7 @@
     picks = np.zeros((256, 384), np.float32)
     picks[:, 0:128] = pick_matrix(SIDE - 1)
     picks[:, 128:256] = pick_matrix(0)
-    return np.concatenate([picks, *shift_matrices(-1), *shift_matrices(1)], axis=0)
+    return np.concatenate([picks, *down_matrices(), *up_matrices()], axis=0)
 
 
 def collect_matrix():
@@ -210,16 +218,6 @@
         return copy
 
     load_x = load(0, x_hbm, x_ref)
-    picks, shifts = pl.ds(0, 256), pl.ds(256, 5376)
-    load_picks = load(1, table_hbm.at[picks], table.at[picks])
-    loads = [
-        load(2, w1_hbm, w1_ref),
-        load(3, spread_hbm, spread_ref),
-        load(4, w2_hbm, w2_ref),
-        load(5, table_hbm.at[shifts], table.at[shifts]),
-        load(6, g_hbm, g_ref),
-        load(7, collect_hbm, collect_ref),
-    ]
 
     def store(n, src, dst):
         copy = pltpu.make_async_copy(src, dst, store_sem.at[n])
@@ -243,11 +241,22 @@
         z_peers.append((p, {"dp": 4 * (p - 2 * high) + x_at, "space": 16 * high + 2 * y + core}))
 
     barrier = pltpu.get_barrier_semaphore()
-    for dims in SUBSETS:
+    for dims in SUBSETS[::-1]:
         for step in (-1, 1):
             pl.semaphore_signal(barrier, inc=1, device_id=neighbour(dims, step), device_id_type=MESH)
-    for _, device in xc_peers + z_peers:
+    for _, device in z_peers + y_peers + xc_peers:
         pl.semaphore_signal(barrier, inc=1, device_id=device, device_id_type=MESH)
+    picks, shifts = pl.ds(0, 256), pl.ds(256, 5376)
+    load_picks = load(1, table_hbm.at[picks], table.at[picks])
+    loads = [
+        load(2, w1_hbm, w1_ref),
+        load(3, spread_hbm, spread_ref),
+        load(4, w2_hbm, w2_ref),
+        load(5, table_hbm.at[shifts], table.at[shifts]),
+        load(6, g_hbm, g_ref),
+        load(7, collect_hbm, collect_ref),
+    ]
+
 
     def rows16(n):
         return pl.ds(pl.multiple_of(16 * n, 16), 16)
@@ -289,9 +298,9 @@
     pieces = split(x, 3)
     picked = dot(pieces[0], pick) + dot(pieces[1], pick) + dot(pieces[2], pick)
     pack([picked[8 * t : 8 * t + 8] for t in range(32)], send, IN_AT, True)
-    pl.semaphore_wait(barrier, 28)
+    pl.semaphore_wait(barrier, 35)
     copies = []
-    for s, dims in enumerate(SUBSETS):
+    for s, dims in reversed(list(enumerate(SUBSETS))):
         rows = pl.ds(IN_AT[s], IN_ROWS[s])
         copies.append(
             pltpu.make_async_remote_copy(
@@ -354,8 +363,8 @@
     def down(s, first, last, lanes):
         return table[256 + 384 * s + first : 256 + 384 * s + last, 0:lanes]
 
-    def up(s, first, last):
-        return table[2944 + 384 * s + first : 2944 + 384 * s + last, 0:256]
+    def up(s, first, last, lanes):
+        return table[2944 + 384 * s + first : 2944 + 384 * s + last, 0:lanes]
 
     def shifted_cells(s):
         places = itertools.product(*[(4,) if d in SUBSETS[s] else range(1, 5) for d in range(3)])
@@ -385,21 +394,21 @@
             xc[at : at + 16, 0:256] += moved[16 * n : 16 * n + 16, 0:256]
             xc[at : at + 16, 256:384] = moved[16 * n : 16 * n + 16, 256:384]
 
-    def stacked(q, lanes):
+    def stacked(q, first, last):
         b = bits(q)
         tiles = []
         for k in range(27):
             at = cell(*[2 * b[d] + offsets(k)[d] for d in range(3)])
-            tiles.append(xc[at : at + 16, 0:lanes])
+            tiles.append(xc[at : at + 16, first:last])
         return jnp.concatenate(tiles, axis=0)
 
     def three(k):
         return 16 * (9 * k[0] + 3 * k[1] + k[2])
 
     for q in range(8):
-        r = dot(one_lhs, stacked(q, 384))
+        r = dot(one_lhs, stacked(q, 0, 384))
         value = (r[32:48] + r[16:32]) + r[0:16]
-        pre[q] = value[:, 0:256]
+        pre[q] = value
         hidden = jnp.where(value > 0, value, SLOPE * value)
         at = three([1 + b for b in bits(q)])
         for n, piece in enumerate(split(hidden, 3)):
@@ -427,11 +436,63 @@
     delta = grad * jnp.where(pre_two > 0, 1.0, SLOPE)
 
     pieces = split(delta, 3)
+    d1, d2 = pieces[0], pieces[1]
+    r = dot_t(hk[0, :, 0:256], d1) + dot_t(hk[0, :, 0:256], d2) + dot_t(hk[1, :, 0:256], d1)
+    r = jnp.concatenate([r, jnp.zeros((16, 32), F32)], axis=0)
+    two_own[0:112, :] = jnp.concatenate([r[112 * n : 112 * n + 112] for n in range(4)], axis=1)
+    two_own[112:128, :] = jnp.zeros((16, 128), F32)
+    two_parts[0, rows16(xc_at), :] = two_own[rows16(xc_at), :]
+    wait_two = exchange(0, xc_at, xc_peers, lambda p: two_own.at[rows16(p)], lambda p: two_parts.at[0, rows16(p)])
+
+    own = jnp.concatenate([d1, d2], axis=0)
+    moved = [jnp.concatenate([own, jnp.zeros((64, 128), BF16)], axis=1)] * 8
+    for s, dims in enumerate(SUBSETS):
+        moved[sum(4 >> d for d in dims)] = dot(own, up(s, 0, 256, 384)).astype(BF16)
+
+    def through_filter(moved):
+        r = dot(back_lhs, jnp.concatenate([m[0:32] for m in moved], axis=0))
+        low = dot(back_lhs[0:128], jnp.concatenate([m[32:64] for m in moved], axis=0))
+        return (r[128:256] + low) + r[0:128]
+
+    given = through_filter(moved)
+    ones = []
+    for q in range(8):
+        value = given[16 * q : 16 * q + 16] * jnp.where(pre[q] > 0, 1.0, SLOPE)
+        ones.append(jnp.concatenate(split(value, 2), axis=0))
+
+    total = None
+    for q in range(8):
+        term = dot_t(stacked(q, 0, 256), ones[q][:, 0:256])
+        total = term if total is None else total + term
+    for pair in ((1, 2), (3, 4), (5, 6), (7,)):
+        left = jnp.concatenate([stacked(q, 256, 384) for q in pair], axis=1)
+        total = total + dot_t(left, jnp.concatenate([ones[q][:, 256:384] for q in pair], axis=1))
+    small = (iota((16, 32), 1) % 16 == iota((16, 32), 0)).astype(BF16)
+    parts = [dot_t(small, piece) for piece in split(total, 3)]
+    r = dot(jnp.concatenate(split((parts[2] + parts[1]) + parts[0], 3), axis=0), collect_ref[...])
+    one_own[0] = (r[32:48] + r[16:32]) + r[0:16]
+
+    def reduce_one(stage, me, peers):
+        one_parts[stage, rows16(me), :] = one_own[stage]
+        return exchange(
+            4 + stage, me, peers, lambda p: one_own.at[stage], lambda p: one_parts.at[stage, rows16(p)]
+        )
+
+    def reduce_two(stage, me, peers):
+        value = sum_of(two_parts.at[stage - 1])
+        two_sum[stage - 1] = value
+        two_parts[stage, rows16(me), :] = value
+        return exchange(
+            stage, me, peers, lambda p: two_sum.at[stage - 1], lambda p: two_parts.at[stage, rows16(p)]
+        )
+
+    wait_one = reduce_one(0, xc_at, xc_peers)
+
     r = dot(jnp.concatenate(pieces, axis=0), table[0:256, 128:256])
     picked = (r[0:32] + r[32:64]) + r[64:96]
     pack([picked[8 * t : 8 * t + 8] for t in range(4)], dsend, D_AT)
     dcopies = []
-    for s, dims in enumerate(SUBSETS):
+    for s, dims in reversed(list(enumerate(SUBSETS))):
         rows = pl.ds(D_AT[s], D_ROWS[s])
         dcopies.append(
             pltpu.make_async_remote_copy(
@@ -445,83 +506,44 @@
         )
         dcopies[-1].start()
 
-    d1, d2 = pieces[0], pieces[1]
-    r = dot_t(hk[0, :, 0:256], d1) + dot_t(hk[0, :, 0:256], d2) + dot_t(hk[1, :, 0:256], d1)
-    r = jnp.concatenate([r, jnp.zeros((16, 32), F32)], axis=0)
-    two_own[0:112, :] = jnp.concatenate([r[112 * n : 112 * n + 112] for n in range(4)], axis=1)
-    two_own[112:128, :] = jnp.zeros((16, 128), F32)
-    two_parts[0, rows16(xc_at), :] = two_own[rows16(xc_at), :]
-    wait_two = exchange(0, xc_at, xc_peers, lambda p: two_own.at[rows16(p)], lambda p: two_parts.at[0, rows16(p)])
-
-    own = jnp.concatenate([d1, d2], axis=0)
-    moved = [own] * 8
-    for s, dims in enumerate(SUBSETS):
-        moved[sum(4 >> d for d in dims)] = dot(own, up(s, 0, 256)).astype(BF16)
+    wait_two()
+    wait_two = reduce_two(1, y, y_peers)
+    wait_one()
+    one_own[1] = sum_of(one_parts.at[0])
+    wait_one = reduce_one(1, y, y_peers)
+    wait_two()
+    wait_two = reduce_two(2, z_at, z_peers)
+    wait_one()
+    one_own[2] = sum_of(one_parts.at[1])
+    wait_one = reduce_one(2, z_at, z_peers)
+
     for copy in dcopies:
         copy.wait_recv()
     higher = flags(3)
     halo = jnp.concatenate([unpack(t, drecv, D_AT, higher) for t in range(4)], axis=0)
     halo = jnp.concatenate(split(halo, 2), axis=0)
+    moved = [jnp.zeros((64, 256), BF16)] * 8
     for s, dims in enumerate(SUBSETS):
-        n = sum(4 >> d for d in dims)
-        moved[n] += dot(halo, up(s, 256, 384)).astype(BF16)
-    da = jnp.concatenate([m[0:32] for m in moved], axis=0)
-    db = jnp.concatenate([m[32:64] for m in moved], axis=0)
-    r = dot(back_lhs, da)
-    r = (r[128:256] + dot(back_lhs[0:128], db)) + r[0:128]
-    ones = []
+        moved[sum(4 >> d for d in dims)] = dot(halo, up(s, 256, 384, 256)).astype(BF16)
+    value = given[:, 0:256] + through_filter(moved)
     for q in range(8):
-        value = r[16 * q : 16 * q + 16]
         for t in range(2):
-            back[t, pl.ds(q, 16, stride=8), :] = value[:, 128 * t : 128 * t + 128]
-        ones.append(jnp.concatenate(split(value * jnp.where(pre[q] > 0, 1.0, SLOPE), 2), axis=0))
+            back[t, pl.ds(q, 16, stride=8), :] = value[16 * q : 16 * q + 16, 128 * t : 128 * t + 128]
     hid_ref[...] = jnp.concatenate([back[0], back[1]], axis=1)[:, 0:CELLS]
     stores.append(store(1, hid_ref, hid_hbm))
 
-    def reduce_two(stage, me, device):
-        value = sum_of(two_parts.at[stage - 1])
-        two_sum[stage - 1] = value
-        two_parts[stage, rows16(me), :] = value
-        return exchange(
-            stage, me, device, lambda p: two_sum.at[stage - 1], lambda p: two_parts.at[stage, rows16(p)]
-        )
-
-    wait_two()
-    wait_two = reduce_two(1, y, y_peers)
-    total = None
-    for q in range(8):
-        term = dot_t(stacked(q, 256), ones[q])
-        total = term if total is None else total + term
-    small = (iota((16, 32), 1) % 16 == iota((16, 32), 0)).astype(F32)
-    one_own[0] = dot(dot_t(small, total, HIGHEST), collect_ref[...], HIGHEST)
-
-    def reduce_one(stage, me, device):
-        one_parts[stage, rows16(me), :] = one_own[stage]
-        return exchange(
-            4 + stage, me, device, lambda p: one_own.at[stage], lambda p: one_parts.at[stage, rows16(p)]
-        )
-
-    wait_one = reduce_one(0, xc_at, xc_peers)
-    wait_two()
-    wait_two = reduce_two(2, z_at, z_peers)
-    wait_one()
-    one_own[1] = sum_of(one_parts.at[0])
-    wait_one = reduce_one(1, y, y_peers)
     wait_two()
     wait_two = reduce_two(3, xc_at, xc_peers)
     wait_one()
-    one_own[2] = sum_of(one_parts.at[1])
-    wait_one = reduce_one(2, z_at, z_peers)
+    value = sum_of(one_parts.at[2])
+    for c in range(4):
+        one_ref[:, c, :] = value[:, 32 * c : 32 * c + 27]
+    stores.append(store(3, one_ref, one_hbm))
     wait_two()
     for n in range(4):
         count = 16 * min(7, 27 - 7 * n)
         two_ref[112 * n : 112 * n + count, :] = two_parts[3, 0:count, 32 * n : 32 * n + 32]
     stores.append(store(2, two_ref, two_hbm))
-    wait_one()
-    value = sum_of(one_parts.at[2])
-    for c in range(4):
-        one_ref[:, c, :] = value[:, 32 * c : 32 * c + 27]
-    stores.append(store(3, one_ref, one_hbm))
     for copy in stores:
         copy.wait()
     for copy in copies + dcopies + sent:
@@ -562,7 +584,7 @@
             pltpu.VMEM((32, CELLS), F32),
             pltpu.VMEM((5632, 384), BF16),
             pltpu.VMEM((27, 432), F32),
-            pltpu.VMEM((432, 128), F32),
+            pltpu.VMEM((432, 128), BF16),
             dma((8,)),
             pltpu.VMEM((32, CELLS), F32),
             pltpu.VMEM((128, CELLS), F32),
@@ -572,7 +594,7 @@
             pltpu.VMEM((3, 512, 128), F32),
             pltpu.VMEM((2000, 384), BF16),
             pltpu.VMEM((3, 432, 384), BF16),
-            pltpu.VMEM((8, 16, 256), F32),
+            pltpu.VMEM((8, 16, 384), F32),
             pltpu.VMEM((2, 128, 128), F32),
             pltpu.VMEM((sum(IN_ROWS), 128), F32),
             pltpu.VMEM((sum(IN_ROWS), 128), F32),
@@ -600,7 +622,7 @@
         out_grad.reshape(32, CELLS),
         jnp.asarray(constant_rows(), BF16),
         jnp.asarray(spread_matrix(), F32),
-        jnp.asarray(collect_matrix(), F32),
+        jnp.asarray(collect_matrix(), BF16),
     )
     level, hidden, grad_one, grad_two = pl.pallas_call(
         finish_kernel,

time: 48.1 us -> 45.6 us (0.948)
  Pallas kernels: 47.3 us -> 44.8 us
    pallas_call x1, Pallas kernels: 45.5 us -> 43 us  [body(): pl.pallas_call(level_kernel, out_shape=shapes, in_specs=[hbm] * 7, out_sp...]
where the time goes in v4:
time: 45.6 us; the launch traced here: 45.4 us
  Pallas kernels  44.8 us (98%)
  between operations  0.64 us (1%)
    pallas_call x1, Pallas kernels, body(): pl.pallas_call(level_kernel, out_shape=shapes, in_specs=[hbm] * 7, out_sp...  43 us
    pallas_call x1, Pallas kernels, body(): pl.pallas_call(finish_kernel, out_shape=shapes, in_specs=[hbm] * 4, out_s...  1.79 us

profile of v4, /device:TPU:1, one launch (start us, length us, event | category | flops | bytes accessed | tf_op | source)
XLA Modules:
  0.0 45.4 jit_solution(5259266260823669651)
XLA Ops:
  0.6 43.0 %shard_map.102 = (f32[32,216]{1,0:T(8,128)}, f32[128,216]{1,0:T(8,128)}, f32[16,4,27]{2,1,0:T(4,128)}, f32[432,32]{1,0:T(8,128)}) custom-call(f32[256,216]{1,0:T(8,128)} %bitcast.14, f32[64,27]{1,0:T(8,128)} %bitcast.16, f32[432,32]{1,0:T(8,128)} %bitcast.15, f32[32,216]{1,0:T(8,128)} %bitcast.17, bf16[5632,384]{1,0:T(8,128)(2,1)} %constant.6.clone.table_hbm, ...), custom_call_target="tpu_custom_call" | custom-call | tf_op jit(solution)/shard_map/pallas_call | solution.py:575
  43.7 1.8 %shard_map.103 = (f32[32,216]{1,0:T(8,128)}, f32[128,216]{1,0:T(8,128)}, f32[16,4,27]{2,1,0:T(4,128)}, f32[432,32]{1,0:T(8,128)}) custom-call(f32[32,216]{1,0:T(8,128)} %get-tuple-element.12.refs_0_, f32[128,216]{1,0:T(8,128)} %get-tuple-element.13.refs_1_, f32[16,4,27]{2,1,0:T(4,128)} %get-tuple-element.14.refs_2_, f32[432,32]{1,0:T(8,128)} %get-tuple-element.15.refs_3_), custom_call_target="tpu_custom_call" | custom-call | tf_op jit(solution)/shard_map/pallas_call | solution.py:627

commit v5 on v4

--- a/solution.py
+++ b/solution.py
@@ -178,9 +178,8 @@
 
 def level_kernel(
     x_hbm, w1_hbm, w2_hbm, g_hbm, table_hbm, spread_hbm, collect_hbm,
-    lev_hbm, hid_hbm, one_hbm, two_hbm,
+    lev_ref, hid_ref, one_ref, two_ref,
     x_ref, w1_ref, w2_ref, g_ref, table, spread_ref, collect_ref, load_sem,
-    lev_ref, hid_ref, one_ref, two_ref, store_sem,
     xs, xc, hk, pre, back, send, recv, dsend, drecv, send_sem, recv_sem, dsend_sem, drecv_sem,
     one_own, one_parts, two_own, two_parts, two_sum, sum_in, sum_out,
 ):
@@ -218,11 +217,6 @@
         return copy
 
     load_x = load(0, x_hbm, x_ref)
-
-    def store(n, src, dst):
-        copy = pltpu.make_async_copy(src, dst, store_sem.at[n])
-        copy.start()
-        return copy
 
     z_lo = lax.div(dp, 4)
     x_at, z_at = dp - 4 * z_lo, 2 * gx + z_lo
@@ -431,7 +425,6 @@
     r3 = dot(two_lhs[0:32], hk[2, :, 0:256])
     pre_two = ((r[64:96] + r2[32:64]) + r3 + (r[32:64] + r2[0:32])) + r[0:32]
     lev_ref[...] = jnp.where(pre_two > 0, pre_two, SLOPE * pre_two)[:, 0:CELLS]
-    stores = [store(0, lev_ref, lev_hbm)]
     grad = jnp.concatenate([g_ref[...], jnp.zeros((32, 40), F32)], axis=1)
     delta = grad * jnp.where(pre_two > 0, 1.0, SLOPE)
 
@@ -530,7 +523,6 @@
         for t in range(2):
             back[t, pl.ds(q, 16, stride=8), :] = value[16 * q : 16 * q + 16, 128 * t : 128 * t + 128]
     hid_ref[...] = jnp.concatenate([back[0], back[1]], axis=1)[:, 0:CELLS]
-    stores.append(store(1, hid_ref, hid_hbm))
 
     wait_two()
     wait_two = reduce_two(3, xc_at, xc_peers)
@@ -538,33 +530,25 @@
     value = sum_of(one_parts.at[2])
     for c in range(4):
         one_ref[:, c, :] = value[:, 32 * c : 32 * c + 27]
-    stores.append(store(3, one_ref, one_hbm))
     wait_two()
     for n in range(4):
         count = 16 * min(7, 27 - 7 * n)
         two_ref[112 * n : 112 * n + count, :] = two_parts[3, 0:count, 32 * n : 32 * n + 32]
-    stores.append(store(2, two_ref, two_hbm))
-    for copy in stores:
-        copy.wait()
     for copy in copies + dcopies + sent:
         copy.wait_send()
 
 
 def finish_kernel(*refs):
-    in_sem, out_sem = refs[-2:]
-    loads = [pltpu.make_async_copy(refs[n], refs[8 + n], in_sem.at[n]) for n in range(4)]
-    stores = [pltpu.make_async_copy(refs[8 + n], refs[4 + n], out_sem.at[n]) for n in range(4)]
-    for copy in loads:
+    copies = [pltpu.make_async_copy(refs[n], refs[4 + n], refs[8].at[n]) for n in range(4)]
+    for copy in copies:
         copy.start()
-    for load, copy in zip(loads, stores):
-        load.wait()
-        copy.start()
-    for copy in stores:
+    for copy in copies:
         copy.wait()
 
 
 def body(volume_in, filter_one, filter_two, out_grad):
     hbm = pl.BlockSpec(memory_space=pltpu.HBM)
+    vmem = pl.BlockSpec(memory_space=pltpu.VMEM)
     dma = pltpu.SemaphoreType.DMA
     shapes = [
         jax.ShapeDtypeStruct((32, CELLS), F32),
@@ -572,11 +556,20 @@
         jax.ShapeDtypeStruct((16, 4, 27), F32),
         jax.ShapeDtypeStruct((432, 32), F32),
     ]
+    operands = (
+        volume_in.reshape(256, CELLS),
+        jnp.transpose(filter_one, (1, 2, 0)).reshape(64, 27),
+        jnp.transpose(filter_two, (0, 2, 1)).reshape(432, 32),
+        out_grad.reshape(32, CELLS),
+        jnp.asarray(constant_rows(), BF16),
+        jnp.asarray(spread_matrix(), F32),
+        jnp.asarray(collect_matrix(), BF16),
+    )
     results = pl.pallas_call(
         level_kernel,
-        out_shape=shapes,
+        out_shape=[pltpu.VMEM(shape.shape, F32) for shape in shapes],
         in_specs=[hbm] * 7,
-        out_specs=[hbm] * 4,
+        out_specs=[vmem] * 4,
         scratch_shapes=[
             pltpu.VMEM((256, CELLS), F32),
             pltpu.VMEM((64, 27), F32),
@@ -586,11 +579,6 @@
             pltpu.VMEM((27, 432), F32),
             pltpu.VMEM((432, 128), BF16),
             dma((8,)),
-            pltpu.VMEM((32, CELLS), F32),
-            pltpu.VMEM((128, CELLS), F32),
-            pltpu.VMEM((16, 4, 27), F32),
-            pltpu.VMEM((432, 32), F32),
-            dma((4,)),
             pltpu.VMEM((3, 512, 128), F32),
             pltpu.VMEM((2000, 384), BF16),
             pltpu.VMEM((3, 432, 384), BF16),
@@ -613,24 +601,16 @@
             dma((7, 8)),
         ],
         compiler_params=pltpu.CompilerParams(
-            collective_id=0, has_side_effects=True, vmem_limit_bytes=60 * 2**20
+            collective_id=0, has_side_effects=True, vmem_limit_bytes=40 * 2**20
         ),
-    )(
-        volume_in.reshape(256, CELLS),
-        jnp.transpose(filter_one, (1, 2, 0)).reshape(64, 27),
-        jnp.transpose(filter_two, (0, 2, 1)).reshape(432, 32),
-        out_grad.reshape(32, CELLS),
-        jnp.asarray(constant_rows(), BF16),
-        jnp.asarray(spread_matrix(), F32),
-        jnp.asarray(collect_matrix(), BF16),
-    )
+    )(*(pltpu.with_memory_space_constraint(operand, pltpu.HBM) for operand in operands))
     level, hidden, grad_one, grad_two = pl.pallas_call(
         finish_kernel,
         out_shape=shapes,
-        in_specs=[hbm] * 4,
+        in_specs=[vmem] * 4,
         out_specs=[hbm] * 4,
-        scratch_shapes=[*(pltpu.VMEM(shape.shape, F32) for shape in shapes), dma((4,)), dma((4,))],
-        compiler_params=pltpu.CompilerParams(vmem_limit_bytes=60 * 2**20),
+        scratch_shapes=[dma((4,))],
+        compiler_params=pltpu.CompilerParams(vmem_limit_bytes=40 * 2**20),
     )(*results)
     return (
         level.reshape(1, 1, 32, CELLS),

time: 45.6 us -> 43.9 us (0.963)
  Pallas kernels: 44.8 us -> 43.1 us
    pallas_call x2, Pallas kernels: 44.8 us -> 43.1 us  [the longest x1 42.3 us: body(): pl.pallas_call(level_kernel, out_shape=[pltpu.VMEM(shape.shape, F32) for...]
where the time goes in v5:
time: 43.9 us; the launch traced here: 43.7 us
  Pallas kernels  43.1 us (98%)
  between operations  0.64 us (1%)
    pallas_call x1, Pallas kernels, body(): pl.pallas_call(level_kernel, out_shape=[pltpu.VMEM(shape.shape, F32) for...  42.3 us

profile of v5, /device:TPU:1, one launch (start us, length us, event | category | flops | bytes accessed | tf_op | source)
XLA Modules:
  0.0 43.7 jit_solution(10340943145668826752)
XLA Ops:
  0.6 42.3 %shard_map.102 = (f32[32,216]{1,0:T(8,128)S(1)}, f32[128,216]{1,0:T(8,128)S(1)}, f32[16,4,27]{2,1,0:T(4,128)S(1)}, f32[432,32]{1,0:T(8,128)S(1)}) custom-call(f32[256,216]{1,0:T(8,128)} %bitcast.14, f32[64,27]{1,0:T(8,128)} %bitcast.16, f32[432,32]{1,0:T(8,128)} %bitcast.15, f32[32,216]{1,0:T(8,128)} %bitcast.17, bf16[5632,384]{1,0:T(8,128)(2,1)} %constant.6.clone.table_hbm, ...), custom_call_target="tpu_custom_call" | custom-call | tf_op jit(solution)/shard_map/pallas_call | solution.py:568
  43.0 0.8 %shard_map.103 = (f32[32,216]{1,0:T(8,128)}, f32[128,216]{1,0:T(8,128)}, f32[16,4,27]{2,1,0:T(4,128)}, f32[432,32]{1,0:T(8,128)}) custom-call(f32[32,216]{1,0:T(8,128)S(1)} %get-tuple-element.12.refs_0_, f32[128,216]{1,0:T(8,128)S(1)} %get-tuple-element.13.refs_1_, f32[16,4,27]{2,1,0:T(4,128)S(1)} %get-tuple-element.14.refs_2_, ...), custom_call_target="tpu_custom_call" | custom-call | tf_op jit(solution)/shard_map/pallas_call | solution.py:607

commit v6 on v5

--- a/solution.py
+++ b/solution.py
@@ -222,14 +222,14 @@
     x_at, z_at = dp - 4 * z_lo, 2 * gx + z_lo
     xc_at = 2 * x_at + core
     xc_peers = []
-    for j in range(4):
+    for j in (2, 1, 3, 0):
         p = wrap(x_at + j, 4)
-        for c in (core, 1 - core):
+        for c in (1 - core, core):
             xc_peers.append((2 * p + c, {"dp": 4 * z_lo + p, "space": 16 * gx + 2 * y + c}))
-    xc_peers = xc_peers[1:]
-    y_peers = [(p, {"space": 16 * gx + 2 * p + core}) for p in (wrap(y + j, 8) for j in range(1, 8))]
+    xc_peers = xc_peers[:-1]
+    y_peers = [(p, {"space": 16 * gx + 2 * p + core}) for p in (wrap(y + j, 8) for j in (4, 3, 5, 2, 6, 1, 7))]
     z_peers = []
-    for j in range(1, 8):
+    for j in (4, 3, 5, 2, 6, 1, 7):
         p = wrap(z_at + j, 8)
         high = lax.div(p, 2)
         z_peers.append((p, {"dp": 4 * (p - 2 * high) + x_at, "space": 16 * high + 2 * y + core}))
@@ -460,11 +460,6 @@
     for pair in ((1, 2), (3, 4), (5, 6), (7,)):
         left = jnp.concatenate([stacked(q, 256, 384) for q in pair], axis=1)
         total = total + dot_t(left, jnp.concatenate([ones[q][:, 256:384] for q in pair], axis=1))
-    small = (iota((16, 32), 1) % 16 == iota((16, 32), 0)).astype(BF16)
-    parts = [dot_t(small, piece) for piece in split(total, 3)]
-    r = dot(jnp.concatenate(split((parts[2] + parts[1]) + parts[0], 3), axis=0), collect_ref[...])
-    one_own[0] = (r[32:48] + r[16:32]) + r[0:16]
-
     def reduce_one(stage, me, peers):
         one_parts[stage, rows16(me), :] = one_own[stage]
         return exchange(
@@ -478,6 +473,13 @@
         return exchange(
             stage, me, peers, lambda p: two_sum.at[stage - 1], lambda p: two_parts.at[stage, rows16(p)]
         )
+
+    wait_two()
+    wait_two = reduce_two(1, y, y_peers)
+    small = (iota((16, 32), 1) % 16 == iota((16, 32), 0)).astype(BF16)
+    parts = [dot_t(small, piece) for piece in split(total, 3)]
+    r = dot(jnp.concatenate(split((parts[2] + parts[1]) + parts[0], 3), axis=0), collect_ref[...])
+    one_own[0] = (r[32:48] + r[16:32]) + r[0:16]
 
     wait_one = reduce_one(0, xc_at, xc_peers)
 
@@ -499,8 +501,6 @@
         )
         dcopies[-1].start()
 
-    wait_two()
-    wait_two = reduce_two(1, y, y_peers)
     wait_one()
     one_own[1] = sum_of(one_parts.at[0])
     wait_one = reduce_one(1, y, y_peers)

time: 43.9 us -> 43.5 us (level)
  no operation moved by 1% of the time
where the time goes in v6:
time: 43.5 us; the launch traced here: 43.4 us
  Pallas kernels  42.7 us (98%)
  between operations  0.64 us (1%)
    pallas_call x1, Pallas kernels, body(): pl.pallas_call(level_kernel, out_shape=[pltpu.VMEM(shape.shape, F32) for...  41.9 us

profile of v6, /device:TPU:1, one launch (start us, length us, event | category | flops | bytes accessed | tf_op | source)
XLA Modules:
  0.0 43.4 jit_solution(14251226553327470691)
XLA Ops:
  0.6 41.9 %shard_map.102 = (f32[32,216]{1,0:T(8,128)S(1)}, f32[128,216]{1,0:T(8,128)S(1)}, f32[16,4,27]{2,1,0:T(4,128)S(1)}, f32[432,32]{1,0:T(8,128)S(1)}) custom-call(f32[256,216]{1,0:T(8,128)} %bitcast.14, f32[64,27]{1,0:T(8,128)} %bitcast.16, f32[432,32]{1,0:T(8,128)} %bitcast.15, f32[32,216]{1,0:T(8,128)} %bitcast.17, bf16[5632,384]{1,0:T(8,128)(2,1)} %constant.6.clone.table_hbm, ...), custom_call_target="tpu_custom_call" | custom-call | tf_op jit(solution)/shard_map/pallas_call | solution.py:568
  42.6 0.8 %shard_map.103 = (f32[32,216]{1,0:T(8,128)}, f32[128,216]{1,0:T(8,128)}, f32[16,4,27]{2,1,0:T(4,128)}, f32[432,32]{1,0:T(8,128)}) custom-call(f32[32,216]{1,0:T(8,128)S(1)} %get-tuple-element.12.refs_0_, f32[128,216]{1,0:T(8,128)S(1)} %get-tuple-element.13.refs_1_, f32[16,4,27]{2,1,0:T(4,128)S(1)} %get-tuple-element.14.refs_2_, ...), custom_call_target="tpu_custom_call" | custom-call | tf_op jit(solution)/shard_map/pallas_call | solution.py:607

commit v7 on v6

--- a/solution.py
+++ b/solution.py
@@ -72,7 +72,7 @@
 
 
 def spread_matrix():
-    m = np.zeros((27, 432), np.float32)
+    m = np.zeros((32, 432), np.float32)
     for k in range(27):
         m[k, 16 * k : 16 * k + 12] = 1
     return m
@@ -148,8 +148,12 @@
             buf[starts[s] + 8 * block : starts[s] + 8 * block + 8, :] = total
 
 
-def unpack(t, buf, starts, valid, trim=False):
+def halo_masks(valid):
     lane = iota((8, 128), 1)
+    return [(lane >= STARTS[s]) & (lane < STARTS[s] + SIZES[s]) & (valid[s] > 0) for s in range(7)]
+
+
+def unpack(t, buf, starts, masks, trim=False):
     total = jnp.zeros((8, 128), F32)
     for s in range(7):
         size = SIZES[s]
@@ -159,8 +163,7 @@
         moved = pltpu.roll(buf[row : row + 8, :], (STARTS[s] - (n % per) * size) % 128, 1)
         if second:
             moved = pltpu.roll(moved, 4 >> s, 0)
-        here = (lane >= STARTS[s]) & (lane < STARTS[s] + size) & (valid[s] > 0)
-        total = jnp.where(here, moved, total)
+        total = jnp.where(masks[s], moved, total)
     return total
 
 
@@ -180,7 +183,7 @@
     x_hbm, w1_hbm, w2_hbm, g_hbm, table_hbm, spread_hbm, collect_hbm,
     lev_ref, hid_ref, one_ref, two_ref,
     x_ref, w1_ref, w2_ref, g_ref, table, spread_ref, collect_ref, load_sem,
-    xs, xc, hk, pre, back, send, recv, dsend, drecv, send_sem, recv_sem, dsend_sem, drecv_sem,
+    xs, xc, xd, hk, pre, back, send, recv, dsend, drecv, send_sem, recv_sem, dsend_sem, drecv_sem,
     one_own, one_parts, two_own, two_parts, two_sum, sum_in, sum_out,
 ):
     dp, where = lax.axis_index("dp"), lax.axis_index("space")
@@ -310,18 +313,19 @@
 
     for copy in loads[0:3]:
         copy.wait()
-    w1 = dot(w1_ref[...], spread_ref[...], HIGHEST)
-    w1 = jnp.where(iota((64, 432), 0) % 4 == iota((64, 432), 1) % 4, w1, 0.0)
-    w1 = dot((iota((16, 64), 1) // 4 == iota((16, 64), 0)).astype(F32), w1, HIGHEST)
+    own_rows = (iota((16, 64), 1) // 4 == iota((16, 64), 0)).astype(BF16)
+    own_lanes = iota((64, 432), 0) % 4 == iota((64, 432), 1) % 4
+    wide = dot(jnp.concatenate(split(w1_ref[...], 3), axis=0), spread_ref[0:27, :])
+    wide = [jnp.where(own_lanes, wide[64 * n : 64 * n + 64], 0.0).astype(BF16) for n in range(3)]
+    w1a, w1b, w1c = [dot(own_rows, piece).astype(BF16) for piece in wide]
     slot = iota((16, 432), 1) // 4 % 4
     zero = jnp.zeros((16, 432), BF16)
-    w1a, w1b, w1c = split(w1, 3)
     large = jnp.where(slot == 0, w1a, zero)
     middle = jnp.where(slot == 0, w1b, jnp.where(slot == 1, w1a, zero))
     least = jnp.where(slot == 0, w1c, jnp.where(slot == 1, w1b, jnp.where(slot == 2, w1a, zero)))
     one_lhs = jnp.concatenate([large, middle, least], axis=0)
-    eye = (iota((32, 32), 0) == iota((32, 32), 1)).astype(F32)
-    two_lhs = jnp.concatenate(split(dot_t(eye, w2_ref[...], HIGHEST), 3), axis=0)
+    eye = (iota((32, 32), 0) == iota((32, 32), 1)).astype(BF16)
+    two_lhs = jnp.concatenate([dot_t(eye, piece).astype(BF16) for piece in split(w2_ref[...], 3)], axis=0)
     back_rows = []
     for q in range(8):
         line = []
@@ -373,9 +377,29 @@
         moved = dot(jnp.concatenate([xc[at : at + 16, 0:256] for at in source], axis=0), down(s, 0, 256, 256)).astype(BF16)
         for n, at in enumerate(target):
             xc[at : at + 16, 0:256] = moved[16 * n : 16 * n + 16]
+    def stacked(q, first, last):
+        b = bits(q)
+        tiles = []
+        for k in range(27):
+            at = cell(*[2 * b[d] + offsets(k)[d] for d in range(3)])
+            tiles.append(xc[at : at + 16, first:last])
+        return jnp.concatenate(tiles, axis=0)
+
+    def level_one(left, right):
+        r = dot(left, right)
+        return (r[32:48] + r[16:32]) + r[0:16]
+
+    shifted, lefts = [], []
+    for q in range(8):
+        pre[q, :, 0:256] = level_one(one_lhs, stacked(q, 0, 256))
+        shifted.append([k for k in range(27) if any(o == 0 and b == 0 for o, b in zip(offsets(k), bits(q)))])
+        if shifted[q]:
+            wide = one_lhs.astype(F32)
+            left = jnp.concatenate([wide[:, 16 * k : 16 * k + 16] for k in shifted[q]], axis=1)
+            lefts.append(left.astype(BF16))
     for copy in copies:
         copy.wait_recv()
-    lower = flags(0)
+    lower = halo_masks(flags(0))
     for t in range(32):
         tile = unpack(t, recv, IN_AT, lower, True)
         xs[2, 8 * t : 8 * t + 8] = tile
@@ -385,23 +409,22 @@
         source, target = shifted_cells(s)
         moved = dot(jnp.concatenate([xc[at : at + 16, 256:384] for at in source], axis=0), down(s, 256, 384, 384)).astype(BF16)
         for n, at in enumerate(target):
-            xc[at : at + 16, 0:256] += moved[16 * n : 16 * n + 16, 0:256]
+            xd[at : at + 16, :] = moved[16 * n : 16 * n + 16, 0:256]
             xc[at : at + 16, 256:384] = moved[16 * n : 16 * n + 16, 256:384]
-
-    def stacked(q, first, last):
-        b = bits(q)
-        tiles = []
-        for k in range(27):
-            at = cell(*[2 * b[d] + offsets(k)[d] for d in range(3)])
-            tiles.append(xc[at : at + 16, first:last])
-        return jnp.concatenate(tiles, axis=0)
 
     def three(k):
         return 16 * (9 * k[0] + 3 * k[1] + k[2])
 
     for q in range(8):
-        r = dot(one_lhs, stacked(q, 0, 384))
-        value = (r[32:48] + r[16:32]) + r[0:16]
+        value = pre[q, :, 0:256]
+        if shifted[q]:
+            tiles = []
+            for k in shifted[q]:
+                at = cell(*[2 * b + o for b, o in zip(bits(q), offsets(k))])
+                tiles.append(xd[at : at + 16, :])
+            value = value + level_one(lefts[q], jnp.concatenate(tiles, axis=0))
+        edge = level_one(one_lhs, stacked(q, 256, 384)) if q else jnp.zeros((16, 128), F32)
+        value = jnp.concatenate([value, edge], axis=1)
         pre[q] = value
         hidden = jnp.where(value > 0, value, SLOPE * value)
         at = three([1 + b for b in bits(q)])
@@ -436,6 +459,10 @@
     two_own[112:128, :] = jnp.zeros((16, 128), F32)
     two_parts[0, rows16(xc_at), :] = two_own[rows16(xc_at), :]
     wait_two = exchange(0, xc_at, xc_peers, lambda p: two_own.at[rows16(p)], lambda p: two_parts.at[0, rows16(p)])
+
+    for s in range(7):
+        for at in shifted_cells(s)[1]:
+            xc[at : at + 16, 0:256] += xd[at : at + 16, :]
 
     own = jnp.concatenate([d1, d2], axis=0)
     moved = [jnp.concatenate([own, jnp.zeros((64, 128), BF16)], axis=1)] * 8
@@ -512,7 +539,7 @@
 
     for copy in dcopies:
         copy.wait_recv()
-    higher = flags(3)
+    higher = halo_masks(flags(3))
     halo = jnp.concatenate([unpack(t, drecv, D_AT, higher) for t in range(4)], axis=0)
     halo = jnp.concatenate(split(halo, 2), axis=0)
     moved = [jnp.zeros((64, 256), BF16)] * 8
@@ -562,7 +589,7 @@
         jnp.transpose(filter_two, (0, 2, 1)).reshape(432, 32),
         out_grad.reshape(32, CELLS),
         jnp.asarray(constant_rows(), BF16),
-        jnp.asarray(spread_matrix(), F32),
+        jnp.asarray(spread_matrix(), BF16),
         jnp.asarray(collect_matrix(), BF16),
     )
     results = pl.pallas_call(
@@ -576,11 +603,12 @@
             pltpu.VMEM((432, 32), F32),
             pltpu.VMEM((32, CELLS), F32),
             pltpu.VMEM((5632, 384), BF16),
-            pltpu.VMEM((27, 432), F32),
+            pltpu.VMEM((32, 432), BF16),
             pltpu.VMEM((432, 128), BF16),
             dma((8,)),
             pltpu.VMEM((3, 512, 128), F32),
             pltpu.VMEM((2000, 384), BF16),
+            pltpu.VMEM((2000, 256), BF16),
             pltpu.VMEM((3, 432, 384), BF16),
             pltpu.VMEM((8, 16, 384), F32),
             pltpu.VMEM((2, 128, 128), F32),

time: 43.5 us -> 43.3 us (level)
  no operation moved by 1% of the time
where the time goes in v7:
time: 43.3 us; the launch traced here: 43.1 us
  Pallas kernels  42.5 us (98%)
  between operations  0.64 us (1%)
    pallas_call x1, Pallas kernels, body(): pl.pallas_call(level_kernel, out_shape=[pltpu.VMEM(shape.shape, F32) for...  41.7 us

profile of v7, /device:TPU:1, one launch (start us, length us, event | category | flops | bytes accessed | tf_op | source)
XLA Modules:
  0.0 43.1 jit_solution(15215767809381206883)
XLA Ops:
  0.6 41.7 %shard_map.102 = (f32[32,216]{1,0:T(8,128)S(1)}, f32[128,216]{1,0:T(8,128)S(1)}, f32[16,4,27]{2,1,0:T(4,128)S(1)}, f32[432,32]{1,0:T(8,128)S(1)}) custom-call(f32[256,216]{1,0:T(8,128)} %bitcast.14, f32[64,27]{1,0:T(8,128)} %bitcast.16, f32[432,32]{1,0:T(8,128)} %bitcast.15, f32[32,216]{1,0:T(8,128)} %bitcast.17, bf16[5632,384]{1,0:T(8,128)(2,1)} %constant.6.clone.table_hbm, ...), custom_call_target="tpu_custom_call" | custom-call | tf_op jit(solution)/shard_map/pallas_call | solution.py:595
  42.3 0.8 %shard_map.103 = (f32[32,216]{1,0:T(8,128)}, f32[128,216]{1,0:T(8,128)}, f32[16,4,27]{2,1,0:T(4,128)}, f32[432,32]{1,0:T(8,128)}) custom-call(f32[32,216]{1,0:T(8,128)S(1)} %get-tuple-element.12.refs_0_, f32[128,216]{1,0:T(8,128)S(1)} %get-tuple-element.13.refs_1_, f32[16,4,27]{2,1,0:T(4,128)S(1)} %get-tuple-element.14.refs_2_, ...), custom_call_target="tpu_custom_call" | custom-call | tf_op jit(solution)/shard_map/pallas_call | solution.py:635

commit v8 on v7

--- a/solution.py
+++ b/solution.py
@@ -241,7 +241,7 @@
     for dims in SUBSETS[::-1]:
         for step in (-1, 1):
             pl.semaphore_signal(barrier, inc=1, device_id=neighbour(dims, step), device_id_type=MESH)
-    for _, device in z_peers + y_peers + xc_peers:
+    for _, device in z_peers[1:3] + z_peers[5:7] + xc_peers[:-1]:
         pl.semaphore_signal(barrier, inc=1, device_id=device, device_id_type=MESH)
     picks, shifts = pl.ds(0, 256), pl.ds(256, 5376)
     load_picks = load(1, table_hbm.at[picks], table.at[picks])
@@ -295,7 +295,7 @@
     pieces = split(x, 3)
     picked = dot(pieces[0], pick) + dot(pieces[1], pick) + dot(pieces[2], pick)
     pack([picked[8 * t : 8 * t + 8] for t in range(32)], send, IN_AT, True)
-    pl.semaphore_wait(barrier, 35)
+    pl.semaphore_wait(barrier, 24)
     copies = []
     for s, dims in reversed(list(enumerate(SUBSETS))):
         rows = pl.ds(IN_AT[s], IN_ROWS[s])

time: 43.3 us -> 42.7 us (0.986)
  Pallas kernels: 42.5 us -> 41.9 us
    pallas_call x1, Pallas kernels: 41.7 us -> 41.1 us  [body(): pl.pallas_call(level_kernel, out_shape=[pltpu.VMEM(shape.shape, F32) for...]
where the time goes in v8:
time: 42.7 us; the launch traced here: 42.6 us
  Pallas kernels  41.9 us (98%)
  between operations  0.64 us (1%)
    pallas_call x1, Pallas kernels, body(): pl.pallas_call(level_kernel, out_shape=[pltpu.VMEM(shape.shape, F32) for...  41.1 us

profile of v8, /device:TPU:1, one launch (start us, length us, event | category | flops | bytes accessed | tf_op | source)
XLA Modules:
  0.0 42.6 jit_solution(6896813793872174052)
XLA Ops:
  0.6 41.1 %shard_map.102 = (f32[32,216]{1,0:T(8,128)S(1)}, f32[128,216]{1,0:T(8,128)S(1)}, f32[16,4,27]{2,1,0:T(4,128)S(1)}, f32[432,32]{1,0:T(8,128)S(1)}) custom-call(f32[256,216]{1,0:T(8,128)} %bitcast.14, f32[64,27]{1,0:T(8,128)} %bitcast.16, f32[432,32]{1,0:T(8,128)} %bitcast.15, f32[32,216]{1,0:T(8,128)} %bitcast.17, bf16[5632,384]{1,0:T(8,128)(2,1)} %constant.6.clone.table_hbm, ...), custom_call_target="tpu_custom_call" | custom-call | tf_op jit(solution)/shard_map/pallas_call | solution.py:595
  41.8 0.8 %shard_map.103 = (f32[32,216]{1,0:T(8,128)}, f32[128,216]{1,0:T(8,128)}, f32[16,4,27]{2,1,0:T(4,128)}, f32[432,32]{1,0:T(8,128)}) custom-call(f32[32,216]{1,0:T(8,128)S(1)} %get-tuple-element.12.refs_0_, f32[128,216]{1,0:T(8,128)S(1)} %get-tuple-element.13.refs_1_, f32[16,4,27]{2,1,0:T(4,128)S(1)} %get-tuple-element.14.refs_2_, ...), custom_call_target="tpu_custom_call" | custom-call | tf_op jit(solution)/shard_map/pallas_call | solution.py:635
